TPU v7x, 128 devices: a whole 4x4x4 slice. The times are simulated.
128 devices in a mesh: users: 8 (over y, core), items: 16 (over z, x).
Axes of the slice: x: 4, y: 4, z: 4, core: 2. Of those that a mesh axis runs over, the one named last changes fastest.
Arguments:
- user_factors: bfloat16 [64, 128, 256], P('users'), may hold values from -1.5 to 1.5
- item_factors: bfloat16 [128, 128, 256], P('items'), may hold values from -1.5 to 1.5
- confidence: bfloat16 [128, 256, 128, 128], P(('users', 'items')), may hold values from 0.25 to 4
- ratings: bfloat16 [128, 256, 128, 128], P(('users', 'items')), may hold values from -6 to 6
- slot_blocks: int32 [128, 16, 2], P(('users', 'items')), may hold values from -1 to 7, as said below
- pair_user: int32 [128, 256], P(('users', 'items')), may hold values from 0 to 7
- pair_slot: int32 [128, 256], P(('users', 'items')), may hold values from 0 to 31, as said below
Outputs:
- user_gradient: float32 [64, 128, 256], P('users')
- item_gradient: float32 [128, 128, 256], P('items')
Inputs may be any that keep to these rules, and one draw needn't show every extreme that they name: `slot_blocks`: each device lists from each owner between 1 and 2 distinct live blocks of 0 to 7, in the first slots, the rest -1. In every draw each row of devices along items lists 2 blocks of one owner from every device, and some slot is empty. `pair_slot`: every pair names a live slot.
All inputs are finite; a program needn't handle non-finite values.
Results may differ from a plain program's by a relative error of at most 0.00045.
Values may be sent and summed in bfloat16 or wider, within the bound.
No kernel may reach another device: no remote copies, remote signals or barrier semaphores. Data moves between devices by JAX's collectives and lax.ppermute only.
A program may use at most 128 MiB of HBM per device.

v0:
```python
import jax
import jax.numpy as jnp
from jax import lax
from jax.sharding import PartitionSpec as P


def accumulate(user_factors, slot_factors, confidence, ratings, pair_user, pair_slot):
    pair_count = pair_user.shape[1]
    group_size = min(64, pair_count)
    turn_count = pair_count // group_size
    tile_size = confidence.shape[2]
    conf_groups = confidence[0].reshape(turn_count, group_size, tile_size, tile_size)
    rate_groups = ratings[0].reshape(turn_count, group_size, tile_size, tile_size)
    user_groups = pair_user[0].reshape(turn_count, group_size)
    slot_groups = pair_slot[0].reshape(turn_count, group_size)

    def advance(carry, inputs):
        acc_user, acc_slot = carry
        conf_tile, rate_tile, user_rows, slot_rows = inputs
        left_tile = user_factors[user_rows]
        right_tile = slot_factors[slot_rows]
        scores = jnp.einsum(
            "pir,pjr->pij", left_tile, right_tile, preferred_element_type=jnp.float32
        )
        weighted = (
            conf_tile.astype(jnp.float32) * (scores - rate_tile.astype(jnp.float32)) / tile_size
        ).astype(jnp.bfloat16)
        user_part = jnp.einsum(
            "pij,pjr->pir", weighted, right_tile, preferred_element_type=jnp.float32
        )
        slot_part = jnp.einsum(
            "pij,pir->pjr", weighted, left_tile, preferred_element_type=jnp.float32
        )
        acc_user = acc_user.at[user_rows].add(user_part)
        acc_slot = acc_slot.at[slot_rows].add(slot_part)
        return ((acc_user, acc_slot), None)

    start = (jnp.zeros(user_factors.shape, jnp.float32), jnp.zeros(slot_factors.shape, jnp.float32))
    (user_grad, slot_grad), _ = lax.scan(
        advance, start, (conf_groups, rate_groups, user_groups, slot_groups)
    )
    return (user_grad, slot_grad)


def body(user_factors, item_factors, confidence, ratings, slot_blocks, pair_user, pair_slot):
    owners = lax.axis_size("items")
    held_blocks = item_factors.shape[0]
    tile_size = item_factors.shape[1]
    rank_width = item_factors.shape[2]
    capacity = slot_blocks.shape[2]
    slot_count = owners * capacity
    wanted = slot_blocks[0]
    owner_base = jnp.arange(owners, dtype=jnp.int32)[:, None] * held_blocks
    flat_ids = jnp.where(wanted >= 0, owner_base + wanted, -1).reshape(slot_count)
    whole = lax.all_gather(item_factors, "items", axis=0, tiled=True)
    slot_factors = whole[jnp.maximum(flat_ids, 0)]
    user_grad, slot_grad = accumulate(
        user_factors, slot_factors, confidence, ratings, pair_user, pair_slot
    )
    user_total = lax.psum(user_grad, "items")
    kept = jnp.where((flat_ids >= 0)[:, None, None], slot_grad, 0.0)
    dense_grad = (
        jnp.zeros((owners * held_blocks, tile_size, rank_width), jnp.float32)
        .at[jnp.maximum(flat_ids, 0)]
        .add(kept)
    )
    owned_grad = lax.psum_scatter(dense_grad, "items", scatter_dimension=0, tiled=True)
    item_total = lax.psum(owned_grad, "users")
    return (user_total, item_total)


def solution(mesh):
    in_specs = (
        P("users", None, None),
        P("items", None, None),
        P(("users", "items"), None, None, None),
        P(("users", "items"), None, None, None),
        P(("users", "items"), None, None),
        P(("users", "items"), None),
        P(("users", "items"), None),
    )
    out_specs = (P("users", None, None), P("items", None, None))
    return jax.shard_map(body, mesh=mesh, in_specs=in_specs, out_specs=out_specs, check_vma=False)
```

profile of v0, /device:TPU:1, one launch (start us, length us, event | category | flops | bytes accessed | tf_op | source)
XLA Modules:
  0.0 636.3 jit_solution(16959855141706460572)
XLA Ops:
  13.1 71.1 %all-gather.2.cloned.1.call-done = bf16[128,128,256]{2,1,0:T(8,128)(2,1)} async-done(((bf16[8,128,256]{2,1,0:T(8,128)(2,1)}), bf16[128,128,256]{2,1,0:T(8,128)(2,1)}) %all-gather.2.cloned.1.call-update) | async-done | bytes 8388624 | tf_op jit(solution)/shard_map/all_gather | solution.py:55
  84.2 5.4 gather_fusion.2
  92.2 246.7 %while.12 = (s32[]{:T(128)}, f32[8,128,256]{2,1,0:T(8,128)S(1)}, f32[32,128,256]{2,1,0:T(8,128)}, s32[4,64]{1,0:T(4,128)S(1)}, bf16[4,64,128,128]{3,2,1,0:T(8,12...) while((s32[]{:T(128)}, f32[8,128,256]{2,1,0:T(8,128)S(1)}, ...), condition=%wide.region_3.4_spmd, body=%wide.region_0.3_spmd.sunk | while | flops 1627392384 | bytes 155200192 | solution.py:39
  92.2 4.4 gather_fusion
  99.4 4.8 fusion.50
  106.3 6.9 %fusion.52 = f32[64,128,256]{2,1,0:T(8,128)} fusion(bf16[64,128,256]{2,1,0:T(8,128)(2,1)S(1)} %copy-done.2, f32[64,128,128]{2,1,0:T(8,128)S(1)} %fusion.50, bf16[4,64,128,128]{3,2,1,0:T(8,128)(2,1)} %get-tuple-element.159, s32[]{:T(128)S(6)} %copy.24, bf16[4,64,128,128]{3,2,1,0:T(8,128)(2,1)} %get-tuple-element.155), kind=kOutput, calls=%fused_computation.10.clone.1 | convolution fusion | flops 543162368 | bytes 20971524 | tf_op jit(solution)/shard_map/while/body/eval_jaxpr/pij,pir->pjr/dot_general | solution.py:31
  113.3 18.9 %scatter_fusion.1 = f32[32,128,256]{2,1,0:T(8,128)} fusion(f32[32,128,256]{2,1,0:T(8,128)} %get-tuple-element.143, s32[64]{0:T(128)S(1)} %get-tuple-element.130, f32[64,128,256]{2,1,0:T(8,128)} %fusion.52), kind=kCustom, calls=%fused_computation.4.clone.1 | custom fusion | flops 2097152 | bytes 25166080 | tf_op jit(solution)/shard_map/while/body/eval_jaxpr/scatter-add | solution.py:35
  132.2 9.2 %fusion.51 = f32[64,128,256]{2,1,0:T(8,128)} fusion(bf16[64,128,256]{2,1,0:T(8,128)(2,1)} %gather_fusion, f32[64,128,128]{2,1,0:T(8,128)} %copy-done.1, bf16[4,64,128,128]{3,2,1,0:T(8,128)(2,1)} %get-tuple-element.159, s32[]{:T(128)S(6)} %copy.24, bf16[4,64,128,128]{3,2,1,0:T(8,128)(2,1)} %get-tuple-element.155), kind=kOutput, calls=%fused_computation.11.clone.1 | convolution fusion | flops 543162368 | bytes 20971524 | tf_op jit(solution)/shard_map/while/body/eval_jaxpr/pij,pjr->pir/dot_general | solution.py:28
  141.4 12.4 %scatter_fusion = f32[8,128,256]{2,1,0:T(8,128)S(1)} fusion(f32[8,128,256]{2,1,0:T(8,128)S(1)} %get-tuple-element.142, s32[64]{0:T(128)S(1)} %get-tuple-element.129, f32[64,128,256]{2,1,0:T(8,128)} %fusion.51), kind=kCustom, calls=%fused_computation.3.clone.1 | custom fusion | flops 2097152 | bytes 25166080 | tf_op jit(solution)/shard_map/while/body/eval_jaxpr/scatter-add | solution.py:34
  153.8 4.4 gather_fusion
  161.0 4.8 fusion.50
  168.0 6.9 %fusion.52 = f32[64,128,256]{2,1,0:T(8,128)} fusion(bf16[64,128,256]{2,1,0:T(8,128)(2,1)S(1)} %copy-done.2, f32[64,128,128]{2,1,0:T(8,128)S(1)} %fusion.50, bf16[4,64,128,128]{3,2,1,0:T(8,128)(2,1)} %get-tuple-element.159, s32[]{:T(128)S(6)} %copy.24, bf16[4,64,128,128]{3,2,1,0:T(8,128)(2,1)} %get-tuple-element.155), kind=kOutput, calls=%fused_computation.10.clone.1 | convolution fusion | flops 543162368 | bytes 20971524 | tf_op jit(solution)/shard_map/while/body/eval_jaxpr/pij,pir->pjr/dot_general | solution.py:31
  174.9 18.9 %scatter_fusion.1 = f32[32,128,256]{2,1,0:T(8,128)} fusion(f32[32,128,256]{2,1,0:T(8,128)} %get-tuple-element.143, s32[64]{0:T(128)S(1)} %get-tuple-element.130, f32[64,128,256]{2,1,0:T(8,128)} %fusion.52), kind=kCustom, calls=%fused_computation.4.clone.1 | custom fusion | flops 2097152 | bytes 25166080 | tf_op jit(solution)/shard_map/while/body/eval_jaxpr/scatter-add | solution.py:35
  193.8 9.2 %fusion.51 = f32[64,128,256]{2,1,0:T(8,128)} fusion(bf16[64,128,256]{2,1,0:T(8,128)(2,1)} %gather_fusion, f32[64,128,128]{2,1,0:T(8,128)} %copy-done.1, bf16[4,64,128,128]{3,2,1,0:T(8,128)(2,1)} %get-tuple-element.159, s32[]{:T(128)S(6)} %copy.24, bf16[4,64,128,128]{3,2,1,0:T(8,128)(2,1)} %get-tuple-element.155), kind=kOutput, calls=%fused_computation.11.clone.1 | convolution fusion | flops 543162368 | bytes 20971524 | tf_op jit(solution)/shard_map/while/body/eval_jaxpr/pij,pjr->pir/dot_general | solution.py:28
  202.9 12.3 %scatter_fusion = f32[8,128,256]{2,1,0:T(8,128)S(1)} fusion(f32[8,128,256]{2,1,0:T(8,128)S(1)} %get-tuple-element.142, s32[64]{0:T(128)S(1)} %get-tuple-element.129, f32[64,128,256]{2,1,0:T(8,128)} %fusion.51), kind=kCustom, calls=%fused_computation.3.clone.1 | custom fusion | flops 2097152 | bytes 25166080 | tf_op jit(solution)/shard_map/while/body/eval_jaxpr/scatter-add | solution.py:34
  215.4 4.4 gather_fusion
  222.6 4.9 fusion.50
  229.5 6.9 %fusion.52 = f32[64,128,256]{2,1,0:T(8,128)} fusion(bf16[64,128,256]{2,1,0:T(8,128)(2,1)S(1)} %copy-done.2, f32[64,128,128]{2,1,0:T(8,128)S(1)} %fusion.50, bf16[4,64,128,128]{3,2,1,0:T(8,128)(2,1)} %get-tuple-element.159, s32[]{:T(128)S(6)} %copy.24, bf16[4,64,128,128]{3,2,1,0:T(8,128)(2,1)} %get-tuple-element.155), kind=kOutput, calls=%fused_computation.10.clone.1 | convolution fusion | flops 543162368 | bytes 20971524 | tf_op jit(solution)/shard_map/while/body/eval_jaxpr/pij,pir->pjr/dot_general | solution.py:31
  236.5 19.1 %scatter_fusion.1 = f32[32,128,256]{2,1,0:T(8,128)} fusion(f32[32,128,256]{2,1,0:T(8,128)} %get-tuple-element.143, s32[64]{0:T(128)S(1)} %get-tuple-element.130, f32[64,128,256]{2,1,0:T(8,128)} %fusion.52), kind=kCustom, calls=%fused_computation.4.clone.1 | custom fusion | flops 2097152 | bytes 25166080 | tf_op jit(solution)/shard_map/while/body/eval_jaxpr/scatter-add | solution.py:35
  255.5 9.2 %fusion.51 = f32[64,128,256]{2,1,0:T(8,128)} fusion(bf16[64,128,256]{2,1,0:T(8,128)(2,1)} %gather_fusion, f32[64,128,128]{2,1,0:T(8,128)} %copy-done.1, bf16[4,64,128,128]{3,2,1,0:T(8,128)(2,1)} %get-tuple-element.159, s32[]{:T(128)S(6)} %copy.24, bf16[4,64,128,128]{3,2,1,0:T(8,128)(2,1)} %get-tuple-element.155), kind=kOutput, calls=%fused_computation.11.clone.1 | convolution fusion | flops 543162368 | bytes 20971524 | tf_op jit(solution)/shard_map/while/body/eval_jaxpr/pij,pjr->pir/dot_general | solution.py:28
  264.7 12.4 %scatter_fusion = f32[8,128,256]{2,1,0:T(8,128)S(1)} fusion(f32[8,128,256]{2,1,0:T(8,128)S(1)} %get-tuple-element.142, s32[64]{0:T(128)S(1)} %get-tuple-element.129, f32[64,128,256]{2,1,0:T(8,128)} %fusion.51), kind=kCustom, calls=%fused_computation.3.clone.1 | custom fusion | flops 2097152 | bytes 25166080 | tf_op jit(solution)/shard_map/while/body/eval_jaxpr/scatter-add | solution.py:34
  284.4 4.8 fusion.50
  291.3 6.9 %fusion.52 = f32[64,128,256]{2,1,0:T(8,128)} fusion(bf16[64,128,256]{2,1,0:T(8,128)(2,1)S(1)} %copy-done.2, f32[64,128,128]{2,1,0:T(8,128)S(1)} %fusion.50, bf16[4,64,128,128]{3,2,1,0:T(8,128)(2,1)} %get-tuple-element.159, s32[]{:T(128)S(6)} %copy.24, bf16[4,64,128,128]{3,2,1,0:T(8,128)(2,1)} %get-tuple-element.155), kind=kOutput, calls=%fused_computation.10.clone.1 | convolution fusion | flops 543162368 | bytes 20971524 | tf_op jit(solution)/shard_map/while/body/eval_jaxpr/pij,pir->pjr/dot_general | solution.py:31
  298.2 19.0 %scatter_fusion.1 = f32[32,128,256]{2,1,0:T(8,128)} fusion(f32[32,128,256]{2,1,0:T(8,128)} %get-tuple-element.143, s32[64]{0:T(128)S(1)} %get-tuple-element.130, f32[64,128,256]{2,1,0:T(8,128)} %fusion.52), kind=kCustom, calls=%fused_computation.4.clone.1 | custom fusion | flops 2097152 | bytes 25166080 | tf_op jit(solution)/shard_map/while/body/eval_jaxpr/scatter-add | solution.py:35
  317.3 9.2 %fusion.51 = f32[64,128,256]{2,1,0:T(8,128)} fusion(bf16[64,128,256]{2,1,0:T(8,128)(2,1)} %gather_fusion, f32[64,128,128]{2,1,0:T(8,128)} %copy-done.1, bf16[4,64,128,128]{3,2,1,0:T(8,128)(2,1)} %get-tuple-element.159, s32[]{:T(128)S(6)} %copy.24, bf16[4,64,128,128]{3,2,1,0:T(8,128)(2,1)} %get-tuple-element.155), kind=kOutput, calls=%fused_computation.11.clone.1 | convolution fusion | flops 543162368 | bytes 20971524 | tf_op jit(solution)/shard_map/while/body/eval_jaxpr/pij,pjr->pir/dot_general | solution.py:28
  326.4 12.4 %scatter_fusion = f32[8,128,256]{2,1,0:T(8,128)S(1)} fusion(f32[8,128,256]{2,1,0:T(8,128)S(1)} %get-tuple-element.142, s32[64]{0:T(128)S(1)} %get-tuple-element.129, f32[64,128,256]{2,1,0:T(8,128)} %fusion.51), kind=kCustom, calls=%fused_computation.3.clone.1 | custom fusion | flops 2097152 | bytes 25166080 | tf_op jit(solution)/shard_map/while/body/eval_jaxpr/scatter-add | solution.py:34
  338.9 5.1 broadcast_select_fusion
  344.0 7.8 %broadcast_in_dim.36 = f32[128,128,256]{2,1,0:T(8,128)} broadcast(f32[]{:T(128)} %constant.17.clone.1), dimensions={} | broadcast | bytes 16777220 | tf_op jit(solution)/shard_map/broadcast_in_dim | solution.py:63
  351.8 9.9 %scatter_fusion.2 = f32[128,128,256]{2,1,0:T(8,128)} fusion(f32[128,128,256]{2,1,0:T(8,128)} %broadcast_in_dim.36, s32[32]{0:T(128)S(1)} %copy-done.5, f32[32,128,256]{2,1,0:T(8,128)} %broadcast_select_fusion), kind=kCustom, calls=%fused_computation.5 | custom fusion | flops 1048576 | bytes 12583040 | tf_op jit(solution)/shard_map/scatter-add | solution.py:65
  362.5 110.2 %reduce-scatter.2.cloned.1.call-done = f32[8,128,256]{2,1,0:T(8,128)} async-done(((f32[128,128,256]{2,1,0:T(8,128)}), f32[8,128,256]{2,1,0:T(8,128)}) %reduce-scatter.2.cloned.1.call-update) | async-done | bytes 1048592 | tf_op jit(solution)/shard_map/reduce_scatter | solution.py:67
  472.7 89.3 %all-reduce.3.cloned.1.call-done = f32[8,128,256]{2,1,0:T(8,128)} async-done(((f32[8,128,256]{2,1,0:T(8,128)}), f32[8,128,256]{2,1,0:T(8,128)}) %all-reduce.3.cloned.1.call-update) | async-done | bytes 1048592 | tf_op jit(solution)/shard_map/psum | solution.py:60
  562.0 63.3 %all-reduce.5.cloned.1.call-done = f32[8,128,256]{2,1,0:T(8,128)} async-done(((f32[8,128,256]{2,1,0:T(8,128)}), f32[8,128,256]{2,1,0:T(8,128)}) %all-reduce.5.cloned.1.call-update) | async-done | bytes 1048592 | tf_op jit(solution)/shard_map/psum | solution.py:68
  (70 shorter events, 37.7 us)
Async XLA Ops:
  7.2 77.1 %all-gather.2.cloned.1.call-start = ((), (), s32[]{:S(2)}) async-start(), calls=%async_computation.1 | async-start | bytes 8912896 | tf_op jit(solution)/shard_map/all_gather | solution.py:55
  7.9 464.8 %reduce-scatter.2.cloned.1.call-start = ((), (), s32[]{:S(2)}) async-start(), calls=%async_computation.3 | async-start | bytes 17825792 | tf_op jit(solution)/shard_map/reduce_scatter | solution.py:67
  12.5 79.6 %copy-start.4 = (s32[32]{0:T(128)}, s32[32]{0:T(128)S(1)}, u32[]{:S(2)}) copy-start(s32[32]{0:T(128)S(1)} %fusion.27) | copy-start | bytes 388
  13.1 79.0 %copy-start.3 = (bf16[8,128,256]{2,1,0:T(8,128)(2,1)S(1)}, bf16[8,128,256]{2,1,0:T(8,128)(2,1)}, u32[]{:S(2)}) copy-start(bf16[8,128,256]{2,1,0:T(8,128)(2,1)} %param.9) | copy-start | bytes 1572868
  92.2 246.7 %copy-start.6 = (pred[32]{0:T(512)(128)(4,1)S(1)}, pred[32]{0:T(512)(128)(4,1)}, u32[]{:S(2)}) copy-start(pred[32]{0:T(512)(128)(4,1)} %fusion.26) | copy-start | bytes 100
  99.4 6.9 %copy-start.2 = (bf16[64,128,256]{2,1,0:T(8,128)(2,1)S(1)}, bf16[64,128,256]{2,1,0:T(8,128)(2,1)}, u32[]{:S(2)}) copy-start(bf16[64,128,256]{2,1,0:T(8,128)(2,1)} %gather_fusion.1) | copy-start | bytes 12582916 | tf_op jit(solution)/shard_map/while
  104.3 2.1 copy-start.1
  161.0 6.9 %copy-start.2 = (bf16[64,128,256]{2,1,0:T(8,128)(2,1)S(1)}, bf16[64,128,256]{2,1,0:T(8,128)(2,1)}, u32[]{:S(2)}) copy-start(bf16[64,128,256]{2,1,0:T(8,128)(2,1)} %gather_fusion.1) | copy-start | bytes 12582916 | tf_op jit(solution)/shard_map/while
  165.9 2.1 copy-start.1
  222.6 6.9 %copy-start.2 = (bf16[64,128,256]{2,1,0:T(8,128)(2,1)S(1)}, bf16[64,128,256]{2,1,0:T(8,128)(2,1)}, u32[]{:S(2)}) copy-start(bf16[64,128,256]{2,1,0:T(8,128)(2,1)} %gather_fusion.1) | copy-start | bytes 12582916 | tf_op jit(solution)/shard_map/while
  227.4 2.1 copy-start.1
  284.4 6.9 %copy-start.2 = (bf16[64,128,256]{2,1,0:T(8,128)(2,1)S(1)}, bf16[64,128,256]{2,1,0:T(8,128)(2,1)}, u32[]{:S(2)}) copy-start(bf16[64,128,256]{2,1,0:T(8,128)(2,1)} %gather_fusion.1) | copy-start | bytes 12582916 | tf_op jit(solution)/shard_map/while
  289.2 2.1 copy-start.1
  338.8 5.1 copy-start
  344.0 7.8 %copy-start.5 = (s32[32]{0:T(128)S(1)}, s32[32]{0:T(128)}, u32[]{:S(2)}) copy-start(s32[32]{0:T(128)} %copy-done.4) | copy-start | bytes 388
  361.7 200.2 %all-reduce.3.cloned.1.call-start = ((), (), s32[]{:S(2)}) async-start(), calls=%async_computation.2 | async-start | bytes 2097152 | tf_op jit(solution)/shard_map/psum | solution.py:60
  362.5 262.8 %all-reduce.5.cloned.1.call-start = ((), (), s32[]{:S(2)}) async-start(), calls=%async_computation.4 | async-start | bytes 2097152 | tf_op jit(solution)/shard_map/psum | solution.py:68
Sparse Core Ops, SparseCore 0:
  10.1 74.0 all-gather.1
  361.8 110.7 reduce-scatter.1
  476.5 85.3 all-reduce.2
  564.2 61.0 all-reduce.4
where the time goes:
time: 639 us; the launch traced here: 636 us
  waiting for transfers between devices  335 us (52%)
  other arithmetic  144 us (23%)
  matrix products  83.8 us (13%)
  local copies, waits for them, and re-layouts  59.3 us (9%)
  between operations  13.8 us (2%)
    reduce_scatter x1, waiting for transfers between devices, body(): lax.psum_scatter(dense_grad, 'items', scatter_dimension=0, tiled=True)  110 us
    psum x1, waiting for transfers between devices, body(): user_total = lax.psum(user_grad, 'items')  89.3 us
    scatter-add x4, other arithmetic, advance(): acc_slot = acc_slot.at[slot_rows].add(slot_part)  75.9 us
    all_gather x1, waiting for transfers between devices, body(): whole = lax.all_gather(item_factors, 'items', axis=0, tiled=True)  71.1 us
    psum x1, waiting for transfers between devices, body(): item_total = lax.psum(owned_grad, 'users')  63.3 us
    scatter-add x4, other arithmetic, advance(): acc_user = acc_user.at[user_rows].add(user_part)  49.5 us
    dot_general x4, matrix products, advance(): jnp.einsum('pij,pjr->pir', weighted, right_tile, preferred_element_type=j...  36.7 us
    dot_general x4, matrix products, advance(): jnp.einsum('pij,pir->pjr', weighted, left_tile, preferred_element_type=jn...  27.8 us
  transfers between devices with their start and end apart: 4, of which 4 were waited for; matrix products, arithmetic and copies ran while one was open for 1% of the time, Pallas kernels for 0%

commit v1 on v0

v1 whole, which is shorter than its diff:
```python
import jax
import jax.numpy as jnp
from jax import lax
from jax.experimental import pallas as pl
from jax.experimental.pallas import tpu as pltpu
from jax.sharding import PartitionSpec as P

F32 = jnp.float32
I16 = jnp.int16
I32 = jnp.int32
META = 16
STEP = 16
LIMIT = 60 * 1024 * 1024


def params():
    return pltpu.CompilerParams(vmem_limit_bytes=LIMIT)


def vmem():
    return pl.BlockSpec(memory_space=pltpu.VMEM)


def smem():
    return pl.BlockSpec(memory_space=pltpu.SMEM)


def encode(x):
    top = jnp.max(jnp.abs(x), axis=0, keepdims=True)
    expo = jnp.ceil(jnp.log2(jnp.maximum(top, 1e-30)) + 1e-4)
    scaled = x * jnp.exp2(14.99 - expo)
    codes = jnp.clip(jnp.round(scaled), -32767.0, 32767.0)
    return codes.astype(I32).astype(I16), expo.astype(I32)


def decode(codes, expo):
    return codes.astype(I32).astype(F32) * jnp.exp2(expo.astype(F32) - 14.99)


def meta_rows(rows):
    width = rows[0].shape[1]
    index = lax.broadcasted_iota(I32, (META, width), 0)
    out = jnp.zeros((META, width), I32)
    for k, row in enumerate(rows):
        out = jnp.where(index == k, row, out)
    return out.astype(I16)


def pick_kernel(ids, blocks, out):
    for i in range(out.shape[0]):
        for q in range(out.shape[1]):
            out[i, q] = blocks[jnp.maximum(ids[i, q], 0)]


def pair_kernel(pu, ps, wanted, conf, rate, users, slots, msg, ugrad, sgrad):
    step = pl.program_id(0)
    count = conf.shape[0]
    tile = conf.shape[1]

    @pl.when(step == 0)
    def _():
        ugrad[...] = jnp.zeros_like(ugrad)
        sgrad[...] = jnp.zeros_like(sgrad)

    for k in range(count):
        b = pu[step * count + k]
        s = ps[step * count + k]
        left = users[b]
        right = slots[s]
        score = lax.dot_general(left, right, (((1,), (1,)), ((), ())), preferred_element_type=F32)
        weighted = (
            conf[k].astype(F32) * (score - rate[k].astype(F32)) * (1.0 / tile)
        ).astype(jnp.bfloat16)
        ugrad[b] += lax.dot_general(
            weighted, right, (((1,), (0,)), ((), ())), preferred_element_type=F32
        )
        sgrad[s] += lax.dot_general(
            weighted, left, (((0,), (0,)), ((), ())), preferred_element_type=F32
        )

    @pl.when(step == pl.num_programs(0) - 1)
    def _():
        owners = msg.shape[0]
        cap = sgrad.shape[0] // owners
        part = (msg.shape[1] - META) - cap * tile
        per = tile // part
        for i in range(owners):
            rows = []
            for q in range(cap):
                codes, expo = encode(sgrad[i * cap + q])
                msg[i, q * tile : (q + 1) * tile] = codes
                rows.append(expo)
            chunk = ugrad[i // per, (i % per) * part : (i % per + 1) * part]
            codes, expo = encode(chunk)
            msg[i, cap * tile : cap * tile + part] = codes
            rows.append(expo)
            msg[i, cap * tile + part :] = meta_rows(rows)


def owner_kernel(ids, got, imsg, umsg, acc):
    owners = got.shape[0]
    held, tile, width = acc.shape
    cap = ids.shape[1]
    part = (got.shape[1] - META) - cap * tile
    acc[...] = jnp.zeros_like(acc)
    total = jnp.zeros((part, width), F32)
    for i in range(owners):
        meta = got[i, cap * tile + part :].astype(I32)
        for q in range(cap):
            block = ids[i, q]
            value = decode(got[i, q * tile : (q + 1) * tile], meta[q : q + 1])

            @pl.when(block >= 0)
            def _():
                acc[block] += value

        total += decode(got[i, cap * tile : cap * tile + part], meta[cap : cap + 1])
    for r in range(held):
        codes, expo = encode(acc[r])
        imsg[r, :tile] = codes
        imsg[r, tile:] = meta_rows([expo])
    codes, expo = encode(total)
    meta = meta_rows([expo])
    for i in range(owners):
        umsg[i, :part] = codes
        umsg[i, part:] = meta


def sum_kernel(got, msg):
    tile = got.shape[1] - META
    total = jnp.zeros((tile, got.shape[2]), F32)
    for r in range(got.shape[0]):
        meta = got[r, tile:].astype(I32)
        total += decode(got[r, :tile], meta[0:1])
    codes, expo = encode(total)
    meta = meta_rows([expo])
    for r in range(got.shape[0]):
        msg[r, :tile] = codes
        msg[r, tile:] = meta


def spread_kernel(got, out):
    part = got.shape[1] - META
    per = out.shape[1] // part
    for r in range(got.shape[0]):
        meta = got[r, part:].astype(I32)
        out[r // per, (r % per) * part : (r % per + 1) * part] = decode(got[r, :part], meta[0:1])


def body(user_factors, item_factors, confidence, ratings, slot_blocks, pair_user, pair_slot):
    owners = lax.axis_size("items")
    rows = lax.axis_size("users")
    held, tile, width = item_factors.shape
    cap = slot_blocks.shape[2]
    count = pair_user.shape[1]
    part = user_factors.shape[0] * tile // owners
    step = min(STEP, count)
    wanted = slot_blocks[0]

    asked = lax.all_to_all(wanted, "items", 0, 0, tiled=True)
    outgoing = pl.pallas_call(
        pick_kernel,
        out_shape=jax.ShapeDtypeStruct((owners, cap, tile, width), item_factors.dtype),
        in_specs=[smem(), vmem()],
        out_specs=vmem(),
        compiler_params=params(),
        name="pick",
    )(asked, item_factors)
    incoming = lax.all_to_all(outgoing, "items", 0, 0, tiled=True)
    slots = incoming.reshape(owners * cap, tile, width)

    depth = cap * tile + part + META
    msg = pl.pallas_call(
        pair_kernel,
        out_shape=jax.ShapeDtypeStruct((owners, depth, width), I16),
        grid_spec=pltpu.PrefetchScalarGridSpec(
            num_scalar_prefetch=3,
            grid=(count // step,),
            in_specs=[
                pl.BlockSpec((step, tile, tile), lambda p, *_: (p, 0, 0)),
                pl.BlockSpec((step, tile, tile), lambda p, *_: (p, 0, 0)),
                vmem(),
                vmem(),
            ],
            out_specs=vmem(),
            scratch_shapes=[
                pltpu.VMEM(user_factors.shape, F32),
                pltpu.VMEM((owners * cap, tile, width), F32),
            ],
        ),
        compiler_params=params(),
        name="pairs",
    )(pair_user[0], pair_slot[0], wanted, confidence[0], ratings[0], user_factors, slots)

    back = lax.all_to_all(msg, "items", 0, 0, tiled=True)
    imsg, umsg = pl.pallas_call(
        owner_kernel,
        out_shape=(
            jax.ShapeDtypeStruct((rows, tile + META, width), I16),
            jax.ShapeDtypeStruct((owners, part + META, width), I16),
        ),
        in_specs=[smem(), vmem()],
        out_specs=(vmem(), vmem()),
        scratch_shapes=[pltpu.VMEM(item_factors.shape, F32)],
        compiler_params=params(),
        name="owners",
    )(asked, back)

    igot = lax.all_to_all(imsg, "users", 0, 0, tiled=True)
    ugot = lax.all_to_all(umsg, "items", 0, 0, tiled=True)
    isum = pl.pallas_call(
        sum_kernel,
        out_shape=jax.ShapeDtypeStruct(igot.shape, I16),
        in_specs=[vmem()],
        out_specs=vmem(),
        compiler_params=params(),
        name="sums",
    )(igot)
    iall = lax.all_to_all(isum, "users", 0, 0, tiled=True)

    def spread(got, shape, name):
        return pl.pallas_call(
            spread_kernel,
            out_shape=jax.ShapeDtypeStruct(shape, F32),
            in_specs=[vmem()],
            out_specs=vmem(),
            compiler_params=params(),
            name=name,
        )(got)

    return (
        spread(ugot, user_factors.shape, "spread_users"),
        spread(iall, item_factors.shape, "spread_items"),
    )


def solution(mesh):
    in_specs = (
        P("users", None, None),
        P("items", None, None),
        P(("users", "items"), None, None, None),
        P(("users", "items"), None, None, None),
        P(("users", "items"), None, None),
        P(("users", "items"), None),
        P(("users", "items"), None),
    )
    out_specs = (P("users", None, None), P("items", None, None))
    return jax.shard_map(body, mesh=mesh, in_specs=in_specs, out_specs=out_specs, check_vma=False)
```

time: 639 us -> 197 us (0.31)
  waiting for transfers between devices: 335 us -> 43.5 us
  other arithmetic: 144 us -> 0 us
  matrix products: 83.8 us -> 0 us
  blocking collectives: 0 us -> 74.3 us
  Pallas kernels: 0 us -> 61.6 us
  local copies, waits for them, and re-layouts: 59.3 us -> 3.58 us
  between operations: 13.8 us -> 0.66 us
  starting transfers between devices: 0.16 us -> 12.8 us
    psum x2 -> x0, waiting for transfers between devices: 153 us -> none  [the longest x1 89.3 us: body(): user_total = lax.psum(user_grad, 'items')]
    scatter-add x9 -> x0, other arithmetic: 135 us -> none  [the longest x4 75.9 us: advance(): acc_slot = acc_slot.at[slot_rows].add(slot_part)]
    reduce_scatter x1 -> x0, waiting for transfers between devices: 110 us -> none  [body(): lax.psum_scatter(dense_grad, 'items', scatter_dimension=0, tiled=True)]
    dot_general x12 -> x0, matrix products: 83.8 us -> none  [the longest x4 36.7 us: advance(): jnp.einsum('pij,pjr->pir', weighted, right_tile, preferred_element_type=j...]
    all_to_all x0 -> x3, blocking collectives: none -> 74.3 us  [the longest x1 41.6 us: body(): back = lax.all_to_all(msg, 'items', 0, 0, tiled=True)]
    all_gather x1 -> x0, waiting for transfers between devices: 71.1 us -> none  [body(): whole = lax.all_gather(item_factors, 'items', axis=0, tiled=True)]
    pallas_call x0 -> x6, Pallas kernels: none -> 61.6 us  [the longest x1 48.7 us: body(): pl.pallas_call(pair_kernel, out_shape=jax.ShapeDtypeStruct((owners, depth...]
    all_to_all x0 -> x3, waiting for transfers between devices: none -> 43.5 us  [the longest x1 25.6 us: body(): incoming = lax.all_to_all(outgoing, 'items', 0, 0, tiled=True)]
  transfers between devices with their start and end apart: 4 -> 3, of which waited for: 4 -> 3; matrix products, arithmetic and copies ran while one was open for 1% -> 0% of each run, Pallas kernels for 0% -> 2%
where the time goes in v1:
time: 197 us; the launch traced here: 196 us
  blocking collectives  74.3 us (38%)
  Pallas kernels  61.6 us (31%)
  waiting for transfers between devices  43.5 us (22%)
  starting transfers between devices  12.8 us (6%)
  local copies, waits for them, and re-layouts  3.58 us (2%)
    pallas_call x1, Pallas kernels, body(): pl.pallas_call(pair_kernel, out_shape=jax.ShapeDtypeStruct((owners, depth...  48.7 us
    all_to_all x1, blocking collectives, body(): back = lax.all_to_all(msg, 'items', 0, 0, tiled=True)  41.6 us
    all_to_all x1, waiting for transfers between devices, body(): incoming = lax.all_to_all(outgoing, 'items', 0, 0, tiled=True)  25.6 us
    all_to_all x1, blocking collectives, body(): igot = lax.all_to_all(imsg, 'users', 0, 0, tiled=True)  18.2 us
    all_to_all x1, blocking collectives, body(): asked = lax.all_to_all(wanted, 'items', 0, 0, tiled=True)  14.6 us
    all_to_all x1, waiting for transfers between devices, body(): ugot = lax.all_to_all(umsg, 'items', 0, 0, tiled=True)  9.87 us
    all_to_all x1, waiting for transfers between devices, body(): iall = lax.all_to_all(isum, 'users', 0, 0, tiled=True)  8.02 us
    all_to_all x1, starting transfers between devices, body(): iall = lax.all_to_all(isum, 'users', 0, 0, tiled=True)  5.32 us
  transfers between devices with their start and end apart: 3, of which 3 were waited for; matrix products, arithmetic and copies ran while one was open for 0% of the time, Pallas kernels for 2%

profile of v1, /device:TPU:1, one launch (start us, length us, event | category | flops | bytes accessed | tf_op | source)
XLA Modules:
  0.0 196.5 jit_solution(10156684320437918577)
XLA Ops:
  0.6 0.8 copy.12
  1.4 14.6 %all_to_all.36 = s32[16,1,2]{2,1,0:T(1,128)} all-to-all(s32[16,1,2]{2,1,0:T(1,128)S(1)} %copy.12), channel_id=1, replica_groups=mesh['users'=8,'items'=16] {'items'}, dimensions={0} | all-to-all | bytes 256 | tf_op jit(solution)/shard_map/all_to_all | solution.py:160
  16.0 2.5 %pick.1 = bf16[16,2,128,256]{3,2,1,0:T(8,128)(2,1)} custom-call(s32[16,2]{1,0:T(8,128)} %bitcast.11, bf16[8,128,256]{2,1,0:T(8,128)(2,1)} %blocks.1), custom_call_target="tpu_custom_call" | custom-call | tf_op jit(solution)/shard_map/pick/pallas_call | solution.py:161
  18.5 0.0 copy-start.3
  18.5 3.8 %all-to-all-start.1 = ((bf16[16,2,128,256]{3,2,1,0:T(8,128)(2,1)}), bf16[16,2,128,256]{3,2,1,0:T(8,128)(2,1)S(1)}, u32[]{:S(2)}, u32[]{:S(2)}) async-start(bf16[16,2,128,256]{3,2,1,0:T(8,128)(2,1)} %pick.1), calls=%async_computation.1 | async-start | bytes 4194304 | tf_op jit(solution)/shard_map/all_to_all | solution.py:169
  22.3 0.0 copy-done.3
  22.4 0.7 copy.15.wanted
  23.0 25.6 %all-to-all-done.1 = bf16[16,2,128,256]{3,2,1,0:T(8,128)(2,1)S(1)} async-done(((bf16[16,2,128,256]{3,2,1,0:T(8,128)(2,1)}), bf16[16,2,128,256]{3,2,1,0:T(8,128)(2,1)S(1)}, u32[]{:S(2)}, u32[]{:S(2)}) %all-to-all-start.1) | async-done | bytes 2097184 | tf_op jit(solution)/shard_map/all_to_all | solution.py:169
  48.7 0.0 copy-start
  48.7 1.3 copy-done
  50.0 48.7 %pairs.1 = s16[16,336,256]{2,1,0:T(8,128)(2,1)} custom-call(s32[256]{0:T(256)} %bitcast.15, s32[256]{0:T(256)} %bitcast.16, s32[16,2]{1,0:T(8,128)} %copy.15.wanted, bf16[256,128,128]{2,1,0:T(8,128)(2,1)} %bitcast.8, bf16[256,128,128]{2,1,0:T(8,128)(2,1)} %bitcast.9, bf16[8,128,256]{2,1,0:T(8,128)(2,1)} %users.1, bf16[32,128,256]{2,1,0:T(8,128)(2,1)} %bitcast.10), custom_call_target="tpu_custom_call" | custom-call | tf_op jit(solution)/shard_map/pairs/pallas_call | solution.py:173
  98.7 41.6 %all_to_all.37.got = s16[16,336,256]{2,1,0:T(8,128)(2,1)} all-to-all(s16[16,336,256]{2,1,0:T(8,128)(2,1)} %pairs.1), channel_id=1, replica_groups=mesh['users'=8,'items'=16] {'items'}, dimensions={0} | all-to-all | bytes 5505024 | tf_op jit(solution)/shard_map/all_to_all | solution.py:195
  140.3 3.9 %owners.1 = (s16[8,144,256]{2,1,0:T(8,128)(2,1)}, s16[16,80,256]{2,1,0:T(8,128)(2,1)}) custom-call(s32[16,2]{1,0:T(8,128)} %bitcast.12, s16[16,336,256]{2,1,0:T(8,128)(2,1)} %all_to_all.37.got), custom_call_target="tpu_custom_call" | custom-call | tf_op jit(solution)/shard_map/owners/pallas_call | solution.py:196
  144.2 18.2 %all_to_all.38.got = s16[8,144,256]{2,1,0:T(8,128)(2,1)} all-to-all(s16[8,144,256]{2,1,0:T(8,128)(2,1)} %get-tuple-element.5), channel_id=1, replica_groups=mesh['users'=8,'items'=16] {'users'}, dimensions={0} | all-to-all | bytes 1179648 | tf_op jit(solution)/shard_map/all_to_all | solution.py:209
  162.4 3.6 %all-to-all-start.3 = ((s16[16,80,256]{2,1,0:T(8,128)(2,1)}), s16[16,80,256]{2,1,0:T(8,128)(2,1)S(1)}, u32[]{:S(2)}, u32[]{:S(2)}) async-start(s16[16,80,256]{2,1,0:T(8,128)(2,1)} %get-tuple-element.4), calls=%async_computation.3 | async-start | bytes 1310720 | tf_op jit(solution)/shard_map/all_to_all | solution.py:210
  166.0 2.1 %sums.1 = s16[8,144,256]{2,1,0:T(8,128)(2,1)} custom-call(s16[8,144,256]{2,1,0:T(8,128)(2,1)} %all_to_all.38.got), custom_call_target="tpu_custom_call" | custom-call | tf_op jit(solution)/shard_map/sums/pallas_call | solution.py:211
  168.1 9.9 %all-to-all-done.3.got = s16[16,80,256]{2,1,0:T(8,128)(2,1)S(1)} async-done(((s16[16,80,256]{2,1,0:T(8,128)(2,1)}), s16[16,80,256]{2,1,0:T(8,128)(2,1)S(1)}, u32[]{:S(2)}, u32[]{:S(2)}) %all-to-all-start.3) | async-done | bytes 655392 | tf_op jit(solution)/shard_map/all_to_all | solution.py:210
  178.0 0.0 copy-start.1
  178.0 5.3 %all-to-all-start.5 = ((s16[8,144,256]{2,1,0:T(8,128)(2,1)}), s16[8,144,256]{2,1,0:T(8,128)(2,1)S(1)}, u32[]{:S(2)}, u32[]{:S(2)}) async-start(s16[8,144,256]{2,1,0:T(8,128)(2,1)} %sums.1), calls=%async_computation.5 | async-start | bytes 1179648 | tf_op jit(solution)/shard_map/all_to_all | solution.py:219
  183.3 0.0 copy-done.1
  183.3 2.2 %spread_users.1 = f32[8,128,256]{2,1,0:T(8,128)} custom-call(s16[16,80,256]{2,1,0:T(8,128)(2,1)} %copy-done.1), custom_call_target="tpu_custom_call" | custom-call | tf_op jit(solution)/shard_map/spread_users/pallas_call | solution.py:222
  185.5 8.0 %all-to-all-done.5.got = s16[8,144,256]{2,1,0:T(8,128)(2,1)S(1)} async-done(((s16[8,144,256]{2,1,0:T(8,128)(2,1)}), s16[8,144,256]{2,1,0:T(8,128)(2,1)S(1)}, u32[]{:S(2)}, u32[]{:S(2)}) %all-to-all-start.5) | async-done | bytes 589856 | tf_op jit(solution)/shard_map/all_to_all | solution.py:219
  193.5 0.0 copy-start.2
  193.5 0.8 copy-done.2
  194.3 2.1 %spread_items.1 = f32[8,128,256]{2,1,0:T(8,128)} custom-call(s16[8,144,256]{2,1,0:T(8,128)(2,1)} %copy-done.2), custom_call_target="tpu_custom_call" | custom-call | tf_op jit(solution)/shard_map/spread_items/pallas_call | solution.py:222
Async XLA Ops:
  18.5 3.9 %copy-start.3 = (s32[1,16,2]{1,2,0:T(2,128)S(1)}, s32[1,16,2]{1,2,0:T(2,128)}, u32[]{:S(2)}) copy-start(s32[1,16,2]{1,2,0:T(2,128)} %param.11) | copy-start | bytes 388
  18.5 30.2 %all-to-all-start.1 = ((bf16[16,2,128,256]{3,2,1,0:T(8,128)(2,1)}), bf16[16,2,128,256]{3,2,1,0:T(8,128)(2,1)S(1)}, u32[]{:S(2)}, u32[]{:S(2)}) async-start(bf16[16,2,128,256]{3,2,1,0:T(8,128)(2,1)} %pick.1), calls=%async_computation.1 | async-start | bytes 4194304 | tf_op jit(solution)/shard_map/all_to_all | solution.py:169
  48.7 1.3 copy-start
  162.4 15.6 %all-to-all-start.3 = ((s16[16,80,256]{2,1,0:T(8,128)(2,1)}), s16[16,80,256]{2,1,0:T(8,128)(2,1)S(1)}, u32[]{:S(2)}, u32[]{:S(2)}) async-start(s16[16,80,256]{2,1,0:T(8,128)(2,1)} %get-tuple-element.4), calls=%async_computation.3 | async-start | bytes 1310720 | tf_op jit(solution)/shard_map/all_to_all | solution.py:210
  178.0 5.3 %copy-start.1 = (s16[16,80,256]{2,1,0:T(8,128)(2,1)}, s16[16,80,256]{2,1,0:T(8,128)(2,1)S(1)}, u32[]{:S(2)}) copy-start(s16[16,80,256]{2,1,0:T(8,128)(2,1)S(1)} %all-to-all-done.3.got) | copy-start | bytes 1966084
  178.0 15.5 %all-to-all-start.5 = ((s16[8,144,256]{2,1,0:T(8,128)(2,1)}), s16[8,144,256]{2,1,0:T(8,128)(2,1)S(1)}, u32[]{:S(2)}, u32[]{:S(2)}) async-start(s16[8,144,256]{2,1,0:T(8,128)(2,1)} %sums.1), calls=%async_computation.5 | async-start | bytes 1179648 | tf_op jit(solution)/shard_map/all_to_all | solution.py:219
  193.5 0.8 copy-start.2

commit v2 on v1

--- a/solution.py
+++ b/solution.py
@@ -9,7 +9,8 @@
 I16 = jnp.int16
 I32 = jnp.int32
 META = 16
-STEP = 16
+STEP = 32
+GROUP = 8
 LIMIT = 60 * 1024 * 1024
 
 
@@ -46,6 +47,10 @@
     return out.astype(I16)
 
 
+def dot(x, y, i, j):
+    return lax.dot_general(x, y, (((i,), (j,)), ((), ())), preferred_element_type=F32)
+
+
 def pick_kernel(ids, blocks, out):
     for i in range(out.shape[0]):
         for q in range(out.shape[1]):
@@ -62,21 +67,22 @@
         ugrad[...] = jnp.zeros_like(ugrad)
         sgrad[...] = jnp.zeros_like(sgrad)
 
-    for k in range(count):
-        b = pu[step * count + k]
-        s = ps[step * count + k]
-        left = users[b]
-        right = slots[s]
-        score = lax.dot_general(left, right, (((1,), (1,)), ((), ())), preferred_element_type=F32)
-        weighted = (
-            conf[k].astype(F32) * (score - rate[k].astype(F32)) * (1.0 / tile)
-        ).astype(jnp.bfloat16)
-        ugrad[b] += lax.dot_general(
-            weighted, right, (((1,), (0,)), ((), ())), preferred_element_type=F32
-        )
-        sgrad[s] += lax.dot_general(
-            weighted, left, (((0,), (0,)), ((), ())), preferred_element_type=F32
-        )
+    for base in range(0, count, GROUP):
+        picks = range(base, base + GROUP)
+        bs = [pu[step * count + k] for k in picks]
+        ss = [ps[step * count + k] for k in picks]
+        lefts = [users[b] for b in bs]
+        rights = [slots[s] for s in ss]
+        scores = [dot(x, y, 1, 1) for x, y in zip(lefts, rights)]
+        tiles = [
+            (conf[k].astype(F32) * (score - rate[k].astype(F32)) * (1.0 / tile)).astype(jnp.bfloat16)
+            for k, score in zip(picks, scores)
+        ]
+        by_user = [dot(w, y, 1, 0) for w, y in zip(tiles, rights)]
+        by_slot = [dot(w, x, 0, 0) for w, x in zip(tiles, lefts)]
+        for b, s, x, y in zip(bs, ss, by_user, by_slot):
+            ugrad[b] += x
+            sgrad[s] += y
 
     @pl.when(step == pl.num_programs(0) - 1)
     def _():
@@ -97,9 +103,10 @@
             msg[i, cap * tile + part :] = meta_rows(rows)
 
 
-def owner_kernel(ids, got, imsg, umsg, acc):
+def owner_kernel(place, ids, got, keep, give, umsg, acc):
     owners = got.shape[0]
     held, tile, width = acc.shape
+    half = held // 2
     cap = ids.shape[1]
     part = (got.shape[1] - META) - cap * tile
     acc[...] = jnp.zeros_like(acc)
@@ -115,10 +122,10 @@
                 acc[block] += value
 
         total += decode(got[i, cap * tile : cap * tile + part], meta[cap : cap + 1])
-    for r in range(held):
-        codes, expo = encode(acc[r])
-        imsg[r, :tile] = codes
-        imsg[r, tile:] = meta_rows([expo])
+    core = place[0]
+    for r in range(half):
+        keep[r] = acc[core * half + r]
+        give[r] = acc[(1 - core) * half + r]
     codes, expo = encode(total)
     meta = meta_rows([expo])
     for i in range(owners):
@@ -126,17 +133,33 @@
         umsg[i, part:] = meta
 
 
-def sum_kernel(got, msg):
-    tile = got.shape[1] - META
-    total = jnp.zeros((tile, got.shape[2]), F32)
-    for r in range(got.shape[0]):
-        meta = got[r, tile:].astype(I32)
-        total += decode(got[r, :tile], meta[0:1])
-    codes, expo = encode(total)
-    meta = meta_rows([expo])
-    for r in range(got.shape[0]):
+def chip_kernel(keep, got, msg):
+    tile = keep.shape[1]
+    for r in range(keep.shape[0]):
+        codes, expo = encode(keep[r] + got[r])
         msg[r, :tile] = codes
-        msg[r, tile:] = meta
+        msg[r, tile:] = meta_rows([expo])
+
+
+def ring_kernel(place, own, one, two, three, out, stack):
+    half, tile, _ = out.shape
+    chips = stack.shape[0]
+    for r in range(half):
+        for k, ref in enumerate((own, one, two, three)):
+            meta = ref[r, tile:].astype(I32)
+            stack[k] = decode(ref[r, :tile], meta[0:1])
+        total = stack[lax.rem(place[1], chips)]
+        for y in range(1, chips):
+            total += stack[lax.rem(place[1] + chips - y, chips)]
+        out[r] = total
+
+
+def join_kernel(place, mine, other, out):
+    half = mine.shape[0]
+    core = place[0]
+    for r in range(half):
+        out[core * half + r] = mine[r]
+        out[(1 - core) * half + r] = other[r]
 
 
 def spread_kernel(got, out):
@@ -193,45 +216,66 @@
     )(pair_user[0], pair_slot[0], wanted, confidence[0], ratings[0], user_factors, slots)
 
     back = lax.all_to_all(msg, "items", 0, 0, tiled=True)
-    imsg, umsg = pl.pallas_call(
+    half = (held // 2, tile, width)
+    row = lax.axis_index("users")
+    place = jnp.stack([row % 2, row // 2]).astype(I32)
+    keep, give, umsg = pl.pallas_call(
         owner_kernel,
         out_shape=(
-            jax.ShapeDtypeStruct((rows, tile + META, width), I16),
+            jax.ShapeDtypeStruct(half, F32),
+            jax.ShapeDtypeStruct(half, F32),
             jax.ShapeDtypeStruct((owners, part + META, width), I16),
         ),
-        in_specs=[smem(), vmem()],
-        out_specs=(vmem(), vmem()),
+        in_specs=[smem(), smem(), vmem()],
+        out_specs=(vmem(), vmem(), vmem()),
         scratch_shapes=[pltpu.VMEM(item_factors.shape, F32)],
         compiler_params=params(),
         name="owners",
-    )(asked, back)
-
-    igot = lax.all_to_all(imsg, "users", 0, 0, tiled=True)
+    )(place, asked, back)
+
+    swap = [(u, u ^ 1) for u in range(rows)]
+    mate = lax.ppermute(give, "users", swap)
+    code = pl.pallas_call(
+        chip_kernel,
+        out_shape=jax.ShapeDtypeStruct((held // 2, tile + META, width), I16),
+        in_specs=[vmem(), vmem()],
+        out_specs=vmem(),
+        compiler_params=params(),
+        name="chip",
+    )(keep, mate)
+    code, umsg = lax.optimization_barrier((code, umsg))
+    ring = [
+        lax.ppermute(code, "users", [(u, (u + 2 * k) % rows) for u in range(rows)])
+        for k in range(1, 4)
+    ]
     ugot = lax.all_to_all(umsg, "items", 0, 0, tiled=True)
-    isum = pl.pallas_call(
-        sum_kernel,
-        out_shape=jax.ShapeDtypeStruct(igot.shape, I16),
+    mine = pl.pallas_call(
+        ring_kernel,
+        out_shape=jax.ShapeDtypeStruct(half, F32),
+        in_specs=[smem()] + [vmem()] * 4,
+        out_specs=vmem(),
+        scratch_shapes=[pltpu.VMEM((4, tile, width), F32)],
+        compiler_params=params(),
+        name="ring",
+    )(place, code, *ring)
+    other = lax.ppermute(mine, "users", swap)
+    item_total = pl.pallas_call(
+        join_kernel,
+        out_shape=jax.ShapeDtypeStruct(item_factors.shape, F32),
+        in_specs=[smem(), vmem(), vmem()],
+        out_specs=vmem(),
+        compiler_params=params(),
+        name="join",
+    )(place, mine, other)
+    user_total = pl.pallas_call(
+        spread_kernel,
+        out_shape=jax.ShapeDtypeStruct(user_factors.shape, F32),
         in_specs=[vmem()],
         out_specs=vmem(),
         compiler_params=params(),
-        name="sums",
-    )(igot)
-    iall = lax.all_to_all(isum, "users", 0, 0, tiled=True)
-
-    def spread(got, shape, name):
-        return pl.pallas_call(
-            spread_kernel,
-            out_shape=jax.ShapeDtypeStruct(shape, F32),
-            in_specs=[vmem()],
-            out_specs=vmem(),
-            compiler_params=params(),
-            name=name,
-        )(got)
-
-    return (
-        spread(ugot, user_factors.shape, "spread_users"),
-        spread(iall, item_factors.shape, "spread_items"),
-    )
+        name="spread",
+    )(ugot)
+    return user_total, item_total
 
 
 def solution(mesh):

time: 197 us -> 160 us (0.81)
  blocking collectives: 74.3 us -> 14.7 us
  waiting for transfers between devices: 43.5 us -> 78.5 us
  Pallas kernels: 61.6 us -> 36.3 us
  starting transfers between devices: 12.8 us -> 20.8 us
  local copies, waits for them, and re-layouts: 3.58 us -> 7.5 us
    all_to_all x2 -> x0, blocking collectives: 59.8 us -> none  [the longest x1 41.6 us: body(): back = lax.all_to_all(msg, 'items', 0, 0, tiled=True)]
    all_to_all x1, waiting for transfers between devices: 8.02 us -> 37.8 us  [body(): back = lax.all_to_all(msg, 'items', 0, 0, tiled=True)]
    pallas_call x1, Pallas kernels: 48.7 us -> 20.9 us  [body(): pl.pallas_call(pair_kernel, out_shape=jax.ShapeDtypeStruct((owners, depth...]
    ppermute x0 -> x5, waiting for transfers between devices: none -> 14.1 us  [the longest x3 12.3 us: body(): lax.ppermute(code, 'users', [(u, (u + 2 * k) % rows) for u in range(rows)])]
    all_to_all x1, waiting for transfers between devices: 9.87 us -> 0.01 us  [body(): ugot = lax.all_to_all(umsg, 'items', 0, 0, tiled=True)]
    ppermute x0 -> x5, starting transfers between devices: none -> 6.97 us  [the longest x3 3.78 us: body(): lax.ppermute(code, 'users', [(u, (u + 2 * k) % rows) for u in range(rows)])]
    unnamed x8 -> x18, local copies, waits for them, and re-layouts: 2.15 us -> 6.06 us
    pallas_call x4 -> x5, Pallas kernels: 10.3 us -> 12.9 us  [the longest x1 3.99 us: body(): pl.pallas_call(owner_kernel, out_shape=(jax.ShapeDtypeStruct(half, F32),...]
  transfers between devices with their start and end apart: 3 -> 8, of which waited for: 3 -> 5; matrix products, arithmetic and copies ran while one was open for 0% -> 1% of each run, Pallas kernels for 2% -> 3%
where the time goes in v2:
time: 160 us; the launch traced here: 159 us
  waiting for transfers between devices  78.5 us (49%)
  Pallas kernels  36.3 us (23%)
  starting transfers between devices  20.8 us (13%)
  blocking collectives  14.7 us (9%)
  local copies, waits for them, and re-layouts  7.5 us (5%)
    all_to_all x1, waiting for transfers between devices, body(): back = lax.all_to_all(msg, 'items', 0, 0, tiled=True)  37.8 us
    all_to_all x1, waiting for transfers between devices, body(): incoming = lax.all_to_all(outgoing, 'items', 0, 0, tiled=True)  26.6 us
    pallas_call x1, Pallas kernels, body(): pl.pallas_call(pair_kernel, out_shape=jax.ShapeDtypeStruct((owners, depth...  20.9 us
    all_to_all x1, blocking collectives, body(): asked = lax.all_to_all(wanted, 'items', 0, 0, tiled=True)  14.7 us
    ppermute x3, waiting for transfers between devices, body(): lax.ppermute(code, 'users', [(u, (u + 2 * k) % rows) for u in range(rows)])  12.3 us
    all_to_all x1, starting transfers between devices, body(): back = lax.all_to_all(msg, 'items', 0, 0, tiled=True)  6.35 us
    unnamed x18, local copies, waits for them, and re-layouts  6.06 us
    pallas_call x1, Pallas kernels, body(): pl.pallas_call(owner_kernel, out_shape=(jax.ShapeDtypeStruct(half, F32),...  3.99 us
  transfers between devices with their start and end apart: 8, of which 5 were waited for; matrix products, arithmetic and copies ran while one was open for 1% of the time, Pallas kernels for 3%

profile of v2, /device:TPU:1, one launch (start us, length us, event | category | flops | bytes accessed | tf_op | source)
XLA Modules:
  0.0 159.2 jit_solution(14051923431196731894)
XLA Ops:
  0.6 0.8 copy.12
  1.4 14.7 %all_to_all.26 = s32[16,1,2]{2,1,0:T(1,128)} all-to-all(s32[16,1,2]{2,1,0:T(1,128)S(1)} %copy.12), channel_id=1, replica_groups=mesh['users'=8,'items'=16] {'items'}, dimensions={0} | all-to-all | bytes 256 | tf_op jit(solution)/shard_map/all_to_all | solution.py:183
  16.1 2.5 %pick.1 = bf16[16,2,128,256]{3,2,1,0:T(8,128)(2,1)} custom-call(s32[16,2]{1,0:T(8,128)} %bitcast.13, bf16[8,128,256]{2,1,0:T(8,128)(2,1)} %blocks.1), custom_call_target="tpu_custom_call" | custom-call | tf_op jit(solution)/shard_map/pick/pallas_call | solution.py:184
  18.6 3.8 %all-to-all-start.1 = ((bf16[16,2,128,256]{3,2,1,0:T(8,128)(2,1)}), bf16[16,2,128,256]{3,2,1,0:T(8,128)(2,1)S(1)}, u32[]{:S(2)}, u32[]{:S(2)}) async-start(bf16[16,2,128,256]{3,2,1,0:T(8,128)(2,1)} %pick.1), calls=%async_computation.1 | async-start | bytes 4194304 | tf_op jit(solution)/shard_map/all_to_all | solution.py:192
  22.5 0.7 copy.15.wanted
  23.2 26.6 %all-to-all-done.1 = bf16[16,2,128,256]{3,2,1,0:T(8,128)(2,1)S(1)} async-done(((bf16[16,2,128,256]{3,2,1,0:T(8,128)(2,1)}), bf16[16,2,128,256]{3,2,1,0:T(8,128)(2,1)S(1)}, u32[]{:S(2)}, u32[]{:S(2)}) %all-to-all-start.1) | async-done | bytes 2097184 | tf_op jit(solution)/shard_map/all_to_all | solution.py:192
  49.8 1.4 copy-done.1
  51.2 20.9 %pairs.1 = s16[16,336,256]{2,1,0:T(8,128)(2,1)} custom-call(s32[256]{0:T(256)} %bitcast.17, s32[256]{0:T(256)} %bitcast.18, s32[16,2]{1,0:T(8,128)} %copy.15.wanted, bf16[256,128,128]{2,1,0:T(8,128)(2,1)} %bitcast.10, bf16[256,128,128]{2,1,0:T(8,128)(2,1)} %bitcast.11, bf16[8,128,256]{2,1,0:T(8,128)(2,1)} %users.1, bf16[32,128,256]{2,1,0:T(8,128)(2,1)} %bitcast.12), custom_call_target="tpu_custom_call" | custom-call | tf_op jit(solution)/shard_map/pairs/pallas_call | solution.py:196
  72.1 6.3 %all-to-all-start.2 = ((s16[16,336,256]{2,1,0:T(8,128)(2,1)}), s16[16,336,256]{2,1,0:T(8,128)(2,1)S(1)}, u32[]{:S(2)}, u32[]{:S(2)}) async-start(s16[16,336,256]{2,1,0:T(8,128)(2,1)} %pairs.1), calls=%async_computation.2 | async-start | bytes 5505024 | tf_op jit(solution)/shard_map/all_to_all | solution.py:218
  78.5 0.6 pad_add_fusion.place
  79.1 37.8 %all-to-all-done.2.got = s16[16,336,256]{2,1,0:T(8,128)(2,1)S(1)} async-done(((s16[16,336,256]{2,1,0:T(8,128)(2,1)}), s16[16,336,256]{2,1,0:T(8,128)(2,1)S(1)}, u32[]{:S(2)}, u32[]{:S(2)}) %all-to-all-start.2) | async-done | bytes 2752544 | tf_op jit(solution)/shard_map/all_to_all | solution.py:218
  117.0 1.5 copy-done
  118.5 4.0 %owners.1 = (f32[4,128,256]{2,1,0:T(8,128)}, f32[4,128,256]{2,1,0:T(8,128)}, s16[16,80,256]{2,1,0:T(8,128)(2,1)}) custom-call(s32[2]{0:T(128)} %pad_add_fusion.place, s32[16,2]{1,0:T(8,128)} %bitcast.14, s16[16,336,256]{2,1,0:T(8,128)(2,1)} %copy-done), custom_call_target="tpu_custom_call" | custom-call | tf_op jit(solution)/shard_map/owners/pallas_call | solution.py:222
  122.5 2.7 %collective-permute-start = (f32[4,128,256]{2,1,0:T(8,128)}, f32[4,128,256]{2,1,0:T(8,128)S(1)}, u32[]{:S(2)}, u32[]{:S(2)}) collective-permute-start(f32[4,128,256]{2,1,0:T(8,128)} %get-tuple-element.8), channel_id=1, source_target_pairs={{0,16},{16,0},{32,48},{48,32},{64,80},{80,64},{96,112},{112,96},{1... | collective-permute-start | bytes 1572872 | tf_op jit(solution)/shard_map/ppermute | solution.py:237
  125.2 1.7 %collective-permute-done.got = f32[4,128,256]{2,1,0:T(8,128)S(1)} collective-permute-done((f32[4,128,256]{2,1,0:T(8,128)}, f32[4,128,256]{2,1,0:T(8,128)S(1)}, u32[]{:S(2)}, u32[]{:S(2)}) %collective-permute-start) | collective-permute-done | bytes 524320 | tf_op jit(solution)/shard_map/ppermute | solution.py:237
  127.0 0.8 copy-done.4
  127.8 2.0 %chip.1.own = s16[4,144,256]{2,1,0:T(8,128)(2,1)} custom-call(f32[4,128,256]{2,1,0:T(8,128)} %get-tuple-element.7.keep, f32[4,128,256]{2,1,0:T(8,128)} %copy-done.4), custom_call_target="tpu_custom_call" | custom-call | tf_op jit(solution)/shard_map/chip/pallas_call | solution.py:238
  129.8 2.7 %collective-permute-start.3 = (s16[4,144,256]{2,1,0:T(8,128)(2,1)}, s16[4,144,256]{2,1,0:T(8,128)(2,1)S(1)}, u32[]{:S(2)}, u32[]{:S(2)}) collective-permute-start(s16[4,144,256]{2,1,0:T(8,128)(2,1)} %chip.1.own), channel_id=1, source_target_pairs={{0,96},{16,112},{32,0},{48,16},{64,32},{80,48},{96,64},{112,80},{1... | collective-permute-start | bytes 884744 | tf_op jit(solution)/shard_map/ppermute | solution.py:248
  132.5 0.3 collective-permute-start.2
  132.9 0.7 collective-permute-start.1
  133.6 3.6 %all-to-all-start.3 = ((s16[16,80,256]{2,1,0:T(8,128)(2,1)}), s16[16,80,256]{2,1,0:T(8,128)(2,1)S(1)}, u32[]{:S(2)}, u32[]{:S(2)}) async-start(s16[16,80,256]{2,1,0:T(8,128)(2,1)} %get-tuple-element.10), calls=%async_computation.3 | async-start | bytes 1310720 | tf_op jit(solution)/shard_map/all_to_all | solution.py:251
  137.2 7.9 %collective-permute-done.3.three = s16[4,144,256]{2,1,0:T(8,128)(2,1)S(1)} collective-permute-done((s16[4,144,256]{2,1,0:T(8,128)(2,1)}, s16[4,144,256]{2,1,0:T(8,128)(2,1)S(1)}, u32[]{:S(2)}, u32[]{:S(2)}) %collective-permute-start.3) | collective-permute-done | bytes 294944 | tf_op jit(solution)/shard_map/ppermute | solution.py:248
  145.0 0.0 collective-permute-done.2.two
  145.1 4.4 %collective-permute-done.1.one = s16[4,144,256]{2,1,0:T(8,128)(2,1)S(1)} collective-permute-done((s16[4,144,256]{2,1,0:T(8,128)(2,1)}, s16[4,144,256]{2,1,0:T(8,128)(2,1)S(1)}, u32[]{:S(2)}, u32[]{:S(2)}) %collective-permute-start.1) | collective-permute-done | bytes 294944 | tf_op jit(solution)/shard_map/ppermute | solution.py:248
  149.5 0.7 copy-done.7
  150.2 2.4 %ring.1.mine = f32[4,128,256]{2,1,0:T(8,128)} custom-call(s32[2]{0:T(128)} %pad_add_fusion.place, s16[4,144,256]{2,1,0:T(8,128)(2,1)} %chip.1.own, s16[4,144,256]{2,1,0:T(8,128)(2,1)} %copy-done.7, s16[4,144,256]{2,1,0:T(8,128)(2,1)} %copy-done.6, s16[4,144,256]{2,1,0:T(8,128)(2,1)} %copy-done.5), custom_call_target="tpu_custom_call" | custom-call | tf_op jit(solution)/shard_map/ring/pallas_call | solution.py:252
  152.6 0.5 collective-permute-start.4
  153.1 0.8 copy-done.2
  154.0 2.2 %spread.1 = f32[8,128,256]{2,1,0:T(8,128)} custom-call(s16[16,80,256]{2,1,0:T(8,128)(2,1)} %copy-done.2), custom_call_target="tpu_custom_call" | custom-call | tf_op jit(solution)/shard_map/spread/pallas_call | solution.py:270
  156.1 0.0 collective-permute-done.4.other
  156.1 0.8 copy-done.3
  156.9 2.2 %join.1 = f32[8,128,256]{2,1,0:T(8,128)} custom-call(s32[2]{0:T(128)} %pad_add_fusion.place, f32[4,128,256]{2,1,0:T(8,128)} %ring.1.mine, f32[4,128,256]{2,1,0:T(8,128)} %copy-done.3), custom_call_target="tpu_custom_call" | custom-call | tf_op jit(solution)/shard_map/join/pallas_call | solution.py:262
  (13 shorter events, 0.0 us)
Async XLA Ops:
  18.6 3.9 %copy-start.8 = (s32[1,16,2]{1,2,0:T(2,128)S(1)}, s32[1,16,2]{1,2,0:T(2,128)}, u32[]{:S(2)}) copy-start(s32[1,16,2]{1,2,0:T(2,128)} %param.11) | copy-start | bytes 388
  18.6 31.2 %all-to-all-start.1 = ((bf16[16,2,128,256]{3,2,1,0:T(8,128)(2,1)}), bf16[16,2,128,256]{3,2,1,0:T(8,128)(2,1)S(1)}, u32[]{:S(2)}, u32[]{:S(2)}) async-start(bf16[16,2,128,256]{3,2,1,0:T(8,128)(2,1)} %pick.1), calls=%async_computation.1 | async-start | bytes 4194304 | tf_op jit(solution)/shard_map/all_to_all | solution.py:192
  49.8 1.4 copy-start.1
  72.1 44.9 %all-to-all-start.2 = ((s16[16,336,256]{2,1,0:T(8,128)(2,1)}), s16[16,336,256]{2,1,0:T(8,128)(2,1)S(1)}, u32[]{:S(2)}, u32[]{:S(2)}) async-start(s16[16,336,256]{2,1,0:T(8,128)(2,1)} %pairs.1), calls=%async_computation.2 | async-start | bytes 5505024 | tf_op jit(solution)/shard_map/all_to_all | solution.py:218
  117.0 1.5 copy-start
  122.5 4.4 %collective-permute-start = (f32[4,128,256]{2,1,0:T(8,128)}, f32[4,128,256]{2,1,0:T(8,128)S(1)}, u32[]{:S(2)}, u32[]{:S(2)}) collective-permute-start(f32[4,128,256]{2,1,0:T(8,128)} %get-tuple-element.8), channel_id=1, source_target_pairs={{0,16},{16,0},{32,48},{48,32},{64,80},{80,64},{96,112},{112,96},{1... | collective-permute-start | bytes 1572872 | tf_op jit(solution)/shard_map/ppermute | solution.py:237
  127.0 0.8 copy-start.4
  129.8 15.2 %collective-permute-start.3 = (s16[4,144,256]{2,1,0:T(8,128)(2,1)}, s16[4,144,256]{2,1,0:T(8,128)(2,1)S(1)}, u32[]{:S(2)}, u32[]{:S(2)}) collective-permute-start(s16[4,144,256]{2,1,0:T(8,128)(2,1)} %chip.1.own), channel_id=1, source_target_pairs={{0,96},{16,112},{32,0},{48,16},{64,32},{80,48},{96,64},{112,80},{1... | collective-permute-start | bytes 884744 | tf_op jit(solution)/shard_map/ppermute | solution.py:248
  132.5 12.5 %collective-permute-start.2 = (s16[4,144,256]{2,1,0:T(8,128)(2,1)}, s16[4,144,256]{2,1,0:T(8,128)(2,1)S(1)}, u32[]{:S(2)}, u32[]{:S(2)}) collective-permute-start(s16[4,144,256]{2,1,0:T(8,128)(2,1)} %chip.1.own), channel_id=1, source_target_pairs={{0,64},{16,80},{32,96},{48,112},{64,0},{80,16},{96,32},{112,48},{1... | collective-permute-start | bytes 884744 | tf_op jit(solution)/shard_map/ppermute | solution.py:248
  132.9 16.6 %collective-permute-start.1 = (s16[4,144,256]{2,1,0:T(8,128)(2,1)}, s16[4,144,256]{2,1,0:T(8,128)(2,1)S(1)}, u32[]{:S(2)}, u32[]{:S(2)}) collective-permute-start(s16[4,144,256]{2,1,0:T(8,128)(2,1)} %chip.1.own), channel_id=1, source_target_pairs={{0,32},{16,48},{32,64},{48,80},{64,96},{80,112},{96,0},{112,16},{1... | collective-permute-start | bytes 884744 | tf_op jit(solution)/shard_map/ppermute | solution.py:248
  133.6 19.5 %all-to-all-start.3 = ((s16[16,80,256]{2,1,0:T(8,128)(2,1)}), s16[16,80,256]{2,1,0:T(8,128)(2,1)S(1)}, u32[]{:S(2)}, u32[]{:S(2)}) async-start(s16[16,80,256]{2,1,0:T(8,128)(2,1)} %get-tuple-element.10), calls=%async_computation.3 | async-start | bytes 1310720 | tf_op jit(solution)/shard_map/all_to_all | solution.py:251
  145.0 4.5 %copy-start.5 = (s16[4,144,256]{2,1,0:T(8,128)(2,1)}, s16[4,144,256]{2,1,0:T(8,128)(2,1)S(1)}, u32[]{:S(2)}) copy-start(s16[4,144,256]{2,1,0:T(8,128)(2,1)S(1)} %collective-permute-done.3.three) | copy-start | bytes 884740
  145.1 4.4 %copy-start.6 = (s16[4,144,256]{2,1,0:T(8,128)(2,1)}, s16[4,144,256]{2,1,0:T(8,128)(2,1)S(1)}, u32[]{:S(2)}) copy-start(s16[4,144,256]{2,1,0:T(8,128)(2,1)S(1)} %collective-permute-done.2.two) | copy-start | bytes 884740
  149.5 0.7 copy-start.7
  152.6 3.5 %collective-permute-start.4 = (f32[4,128,256]{2,1,0:T(8,128)}, f32[4,128,256]{2,1,0:T(8,128)S(1)}, u32[]{:S(2)}, u32[]{:S(2)}) collective-permute-start(f32[4,128,256]{2,1,0:T(8,128)} %ring.1.mine), channel_id=1, source_target_pairs={{0,16},{16,0},{32,48},{48,32},{64,80},{80,64},{96,112},{112,96},{1... | collective-permute-start | bytes 1572872 | tf_op jit(solution)/shard_map/ppermute | solution.py:261
  153.1 0.8 copy-start.2
  156.1 0.8 copy-start.3

commit v3 on v2

--- a/solution.py
+++ b/solution.py
@@ -11,7 +11,7 @@
 META = 16
 STEP = 32
 GROUP = 8
-LIMIT = 60 * 1024 * 1024
+LIMIT = 32 * 1024 * 1024
 
 
 def params():
@@ -20,6 +20,18 @@
 
 def vmem():
     return pl.BlockSpec(memory_space=pltpu.VMEM)
+
+
+def near(x):
+    return pltpu.with_memory_space_constraint(x, pltpu.VMEM)
+
+
+def far(x):
+    return pltpu.with_memory_space_constraint(x, pltpu.HBM)
+
+
+def made(shape, dtype):
+    return pltpu.VMEM(shape, dtype)
 
 
 def smem():
@@ -183,19 +195,19 @@
     asked = lax.all_to_all(wanted, "items", 0, 0, tiled=True)
     outgoing = pl.pallas_call(
         pick_kernel,
-        out_shape=jax.ShapeDtypeStruct((owners, cap, tile, width), item_factors.dtype),
+        out_shape=pltpu.HBM((owners, cap, tile, width), item_factors.dtype),
         in_specs=[smem(), vmem()],
         out_specs=vmem(),
         compiler_params=params(),
         name="pick",
     )(asked, item_factors)
     incoming = lax.all_to_all(outgoing, "items", 0, 0, tiled=True)
-    slots = incoming.reshape(owners * cap, tile, width)
+    slots = near(incoming.reshape(owners * cap, tile, width))
 
     depth = cap * tile + part + META
     msg = pl.pallas_call(
         pair_kernel,
-        out_shape=jax.ShapeDtypeStruct((owners, depth, width), I16),
+        out_shape=pltpu.HBM((owners, depth, width), I16),
         grid_spec=pltpu.PrefetchScalarGridSpec(
             num_scalar_prefetch=3,
             grid=(count // step,),
@@ -213,7 +225,7 @@
         ),
         compiler_params=params(),
         name="pairs",
-    )(pair_user[0], pair_slot[0], wanted, confidence[0], ratings[0], user_factors, slots)
+    )(pair_user[0], pair_slot[0], wanted, far(confidence[0]), far(ratings[0]), user_factors, slots)
 
     back = lax.all_to_all(msg, "items", 0, 0, tiled=True)
     half = (held // 2, tile, width)
@@ -222,27 +234,27 @@
     keep, give, umsg = pl.pallas_call(
         owner_kernel,
         out_shape=(
-            jax.ShapeDtypeStruct(half, F32),
-            jax.ShapeDtypeStruct(half, F32),
-            jax.ShapeDtypeStruct((owners, part + META, width), I16),
+            made(half, F32),
+            made(half, F32),
+            pltpu.HBM((owners, part + META, width), I16),
         ),
         in_specs=[smem(), smem(), vmem()],
         out_specs=(vmem(), vmem(), vmem()),
         scratch_shapes=[pltpu.VMEM(item_factors.shape, F32)],
         compiler_params=params(),
         name="owners",
-    )(place, asked, back)
+    )(place, asked, near(back))
 
     swap = [(u, u ^ 1) for u in range(rows)]
     mate = lax.ppermute(give, "users", swap)
     code = pl.pallas_call(
         chip_kernel,
-        out_shape=jax.ShapeDtypeStruct((held // 2, tile + META, width), I16),
+        out_shape=made((held // 2, tile + META, width), I16),
         in_specs=[vmem(), vmem()],
         out_specs=vmem(),
         compiler_params=params(),
         name="chip",
-    )(keep, mate)
+    )(near(keep), near(mate))
     code, umsg = lax.optimization_barrier((code, umsg))
     ring = [
         lax.ppermute(code, "users", [(u, (u + 2 * k) % rows) for u in range(rows)])
@@ -251,13 +263,13 @@
     ugot = lax.all_to_all(umsg, "items", 0, 0, tiled=True)
     mine = pl.pallas_call(
         ring_kernel,
-        out_shape=jax.ShapeDtypeStruct(half, F32),
+        out_shape=made(half, F32),
         in_specs=[smem()] + [vmem()] * 4,
         out_specs=vmem(),
         scratch_shapes=[pltpu.VMEM((4, tile, width), F32)],
         compiler_params=params(),
         name="ring",
-    )(place, code, *ring)
+    )(place, near(code), *[near(x) for x in ring])
     other = lax.ppermute(mine, "users", swap)
     item_total = pl.pallas_call(
         join_kernel,
@@ -266,7 +278,7 @@
         out_specs=vmem(),
         compiler_params=params(),
         name="join",
-    )(place, mine, other)
+    )(place, near(mine), near(other))
     user_total = pl.pallas_call(
         spread_kernel,
         out_shape=jax.ShapeDtypeStruct(user_factors.shape, F32),
@@ -274,7 +286,7 @@
         out_specs=vmem(),
         compiler_params=params(),
         name="spread",
-    )(ugot)
+    )(near(ugot))
     return user_total, item_total
 
 

time: 160 us -> 147 us (0.919)
  Pallas kernels: 36.3 us -> 29 us
  local copies, waits for them, and re-layouts: 7.5 us -> 1.9 us
    pallas_call x5, Pallas kernels: 31.9 us -> 26.3 us  [the longest x1 20.6 us: body(): pl.pallas_call(pair_kernel, out_shape=pltpu.HBM((owners, depth, width), I...]
    unnamed x18 -> x10, local copies, waits for them, and re-layouts: 6.06 us -> 1.06 us
  transfers between devices with their start and end apart: 8 -> 8, of which waited for: 5 -> 6; matrix products, arithmetic and copies ran while one was open for 1% -> 0% of each run, Pallas kernels for 3% -> 1%
where the time goes in v3:
time: 147 us
  waiting for transfers between devices  79.3 us (54%)
  Pallas kernels  29 us (20%)
  starting transfers between devices  21.4 us (15%)
  blocking collectives  14.6 us (10%)
  local copies, waits for them, and re-layouts  1.9 us (1%)
    all_to_all x1, waiting for transfers between devices, body(): back = lax.all_to_all(msg, 'items', 0, 0, tiled=True)  38.4 us
    all_to_all x1, waiting for transfers between devices, body(): incoming = lax.all_to_all(outgoing, 'items', 0, 0, tiled=True)  26.7 us
    pallas_call x1, Pallas kernels, body(): pl.pallas_call(pair_kernel, out_shape=pltpu.HBM((owners, depth, width), I...  20.6 us
    all_to_all x1, blocking collectives, body(): asked = lax.all_to_all(wanted, 'items', 0, 0, tiled=True)  14.6 us
    ppermute x3, waiting for transfers between devices, body(): lax.ppermute(code, 'users', [(u, (u + 2 * k) % rows) for u in range(rows)])  12.2 us
    all_to_all x1, starting transfers between devices, body(): back = lax.all_to_all(msg, 'items', 0, 0, tiled=True)  6.8 us
    ppermute x3, starting transfers between devices, body(): lax.ppermute(code, 'users', [(u, (u + 2 * k) % rows) for u in range(rows)])  3.87 us
    all_to_all x1, starting transfers between devices, body(): incoming = lax.all_to_all(outgoing, 'items', 0, 0, tiled=True)  3.86 us
  transfers between devices with their start and end apart: 8, of which 6 were waited for; matrix products, arithmetic and copies ran while one was open for 0% of the time, Pallas kernels for 1%

profile of v3, /device:TPU:1, one launch (start us, length us, event | category | flops | bytes accessed | tf_op | source)
XLA Modules:
  0.0 147.0 jit_solution(8313010086853847119)
XLA Ops:
  0.6 0.8 copy.12
  1.4 14.6 %all_to_all.26 = s32[16,1,2]{2,1,0:T(1,128)S(1)} all-to-all(s32[16,1,2]{2,1,0:T(1,128)S(1)} %copy.12), channel_id=1, replica_groups=mesh['users'=8,'items'=16] {'items'}, dimensions={0} | all-to-all | bytes 256 | tf_op jit(solution)/shard_map/all_to_all | solution.py:195
  16.0 1.0 copy-done
  17.1 2.1 %pick.1 = bf16[16,2,128,256]{3,2,1,0:T(8,128)(2,1)} custom-call(s32[16,2]{1,0:T(8,128)S(1)} %bitcast.11, bf16[8,128,256]{2,1,0:T(8,128)(2,1)S(1)} %copy-done), custom_call_target="tpu_custom_call" | custom-call | tf_op jit(solution)/shard_map/pick/pallas_call | solution.py:196
  19.2 3.9 %all-to-all-start.1 = ((bf16[16,2,128,256]{3,2,1,0:T(8,128)(2,1)}), bf16[16,2,128,256]{3,2,1,0:T(8,128)(2,1)S(1)}, u32[]{:S(2)}, u32[]{:S(2)}) async-start(bf16[16,2,128,256]{3,2,1,0:T(8,128)(2,1)} %pick.1), calls=%async_computation.1 | async-start | bytes 4194304 | tf_op jit(solution)/shard_map/all_to_all | solution.py:204
  23.1 0.0 copy-done.4
  23.1 0.1 copy.15.wanted
  23.2 26.7 %all-to-all-done.1 = bf16[16,2,128,256]{3,2,1,0:T(8,128)(2,1)S(1)} async-done(((bf16[16,2,128,256]{3,2,1,0:T(8,128)(2,1)}), bf16[16,2,128,256]{3,2,1,0:T(8,128)(2,1)S(1)}, u32[]{:S(2)}, u32[]{:S(2)}) %all-to-all-start.1) | async-done | bytes 2097184 | tf_op jit(solution)/shard_map/all_to_all | solution.py:204
  49.9 0.0 copy-done.1
  49.9 0.0 copy-done.2
  49.9 0.0 copy-done.3
  49.9 20.6 %pairs.1 = s16[16,336,256]{2,1,0:T(8,128)(2,1)} custom-call(s32[256]{0:T(256)S(1)} %bitcast.13, s32[256]{0:T(256)S(1)} %bitcast.14, s32[16,2]{1,0:T(8,128)S(1)} %copy.15.wanted, bf16[256,128,128]{2,1,0:T(8,128)(2,1)} %bitcast.15, bf16[256,128,128]{2,1,0:T(8,128)(2,1)} %bitcast.16, bf16[8,128,256]{2,1,0:T(8,128)(2,1)S(1)} %copy-done.1, ...), custom_call_target="tpu_custom_call" | custom-call | tf_op jit(solution)/shard_map/pairs/pallas_call | solution.py:208
  70.5 6.8 %all-to-all-start.2 = ((s16[16,336,256]{2,1,0:T(8,128)(2,1)}), s16[16,336,256]{2,1,0:T(8,128)(2,1)S(1)}, u32[]{:S(2)}, u32[]{:S(2)}) async-start(s16[16,336,256]{2,1,0:T(8,128)(2,1)} %pairs.1), calls=%async_computation.2 | async-start | bytes 5505024 | tf_op jit(solution)/shard_map/all_to_all | solution.py:230
  77.3 0.1 pad_add_fusion.place
  77.4 38.4 %all-to-all-done.2.got = s16[16,336,256]{2,1,0:T(8,128)(2,1)S(1)} async-done(((s16[16,336,256]{2,1,0:T(8,128)(2,1)}), s16[16,336,256]{2,1,0:T(8,128)(2,1)S(1)}, u32[]{:S(2)}, u32[]{:S(2)}) %all-to-all-start.2) | async-done | bytes 2752544 | tf_op jit(solution)/shard_map/all_to_all | solution.py:230
  115.8 2.5 %owners.1 = (f32[4,128,256]{2,1,0:T(8,128)S(1)}, f32[4,128,256]{2,1,0:T(8,128)S(1)}, s16[16,80,256]{2,1,0:T(8,128)(2,1)}) custom-call(s32[2]{0:T(128)S(1)} %pad_add_fusion.place, s32[16,2]{1,0:T(8,128)S(1)} %bitcast.12, s16[16,336,256]{2,1,0:T(8,128)(2,1)S(1)} %all-to-all-done.2.got), custom_call_target="tpu_custom_call" | custom-call | tf_op jit(solution)/shard_map/owners/pallas_call | solution.py:234
  118.3 2.7 %collective-permute-start = (f32[4,128,256]{2,1,0:T(8,128)S(1)}, f32[4,128,256]{2,1,0:T(8,128)S(1)}, u32[]{:S(2)}, u32[]{:S(2)}) collective-permute-start(f32[4,128,256]{2,1,0:T(8,128)S(1)} %get-tuple-element.8), channel_id=1, source_target_pairs={{0,16},{16,0},{32,48},{48,32},{64,80},{80,64},{96,112},{112,96},{1... | collective-permute-start | bytes 1572872 | tf_op jit(solution)/shard_map/ppermute | solution.py:249
  121.0 1.5 %collective-permute-done.got = f32[4,128,256]{2,1,0:T(8,128)S(1)} collective-permute-done((f32[4,128,256]{2,1,0:T(8,128)S(1)}, f32[4,128,256]{2,1,0:T(8,128)S(1)}, u32[]{:S(2)}, u32[]{:S(2)}) %collective-permute-start) | collective-permute-done | bytes 524320 | tf_op jit(solution)/shard_map/ppermute | solution.py:249
  122.5 0.1 chip.1.own
  122.7 2.9 %collective-permute-start.3 = (s16[4,144,256]{2,1,0:T(8,128)(2,1)S(1)}, s16[4,144,256]{2,1,0:T(8,128)(2,1)S(1)}, u32[]{:S(2)}, u32[]{:S(2)}) collective-permute-start(s16[4,144,256]{2,1,0:T(8,128)(2,1)S(1)} %chip.1.own), channel_id=1, source_target_pairs={{0,96},{16,112},{32,0},{48,16},{64,32},{80,48},{96,64},{112,80},{1... | collective-permute-start | bytes 884744 | tf_op jit(solution)/shard_map/ppermute | solution.py:260
  125.6 0.3 collective-permute-start.2
  125.9 0.6 collective-permute-start.1
  126.6 3.6 %all-to-all-start.3 = ((s16[16,80,256]{2,1,0:T(8,128)(2,1)}), s16[16,80,256]{2,1,0:T(8,128)(2,1)S(1)}, u32[]{:S(2)}, u32[]{:S(2)}) async-start(s16[16,80,256]{2,1,0:T(8,128)(2,1)} %get-tuple-element.10), calls=%async_computation.3 | async-start | bytes 1310720 | tf_op jit(solution)/shard_map/all_to_all | solution.py:263
  130.2 7.7 %collective-permute-done.3.three = s16[4,144,256]{2,1,0:T(8,128)(2,1)S(1)} collective-permute-done((s16[4,144,256]{2,1,0:T(8,128)(2,1)S(1)}, s16[4,144,256]{2,1,0:T(8,128)(2,1)S(1)}, u32[]{:S(2)}, u32[]{:S(2)}) %collective-permute-start.3) | collective-permute-done | bytes 294944 | tf_op jit(solution)/shard_map/ppermute | solution.py:260
  137.8 0.0 collective-permute-done.2.two
  137.8 4.6 %collective-permute-done.1.one = s16[4,144,256]{2,1,0:T(8,128)(2,1)S(1)} collective-permute-done((s16[4,144,256]{2,1,0:T(8,128)(2,1)S(1)}, s16[4,144,256]{2,1,0:T(8,128)(2,1)S(1)}, u32[]{:S(2)}, u32[]{:S(2)}) %collective-permute-start.1) | collective-permute-done | bytes 294944 | tf_op jit(solution)/shard_map/ppermute | solution.py:260
  142.4 0.9 ring.1.mine
  143.3 0.6 collective-permute-start.4
  143.9 0.0 all-to-all-done.3.got
  143.9 1.1 spread.1
  145.0 0.4 collective-permute-done.4.other
  145.4 1.6 %join.1 = f32[8,128,256]{2,1,0:T(8,128)} custom-call(s32[2]{0:T(128)S(1)} %pad_add_fusion.place, f32[4,128,256]{2,1,0:T(8,128)S(1)} %ring.1.mine, f32[4,128,256]{2,1,0:T(8,128)S(1)} %collective-permute-done.4.other), custom_call_target="tpu_custom_call" | custom-call | tf_op jit(solution)/shard_map/join/pallas_call | solution.py:274
  (5 shorter events, 0.0 us)
Async XLA Ops:
  16.0 1.0 copy-start
  19.2 3.9 %copy-start.4 = (s32[1,16,2]{1,2,0:T(2,128)S(1)}, s32[1,16,2]{1,2,0:T(2,128)}, u32[]{:S(2)}) copy-start(s32[1,16,2]{1,2,0:T(2,128)} %param.11) | copy-start | bytes 388
  19.2 30.7 %copy-start.1 = (bf16[8,128,256]{2,1,0:T(8,128)(2,1)S(1)}, bf16[8,128,256]{2,1,0:T(8,128)(2,1)}, u32[]{:S(2)}) copy-start(bf16[8,128,256]{2,1,0:T(8,128)(2,1)} %users.1) | copy-start | bytes 1572868
  19.2 30.7 %copy-start.2 = (s32[1,256]{1,0:T(1,128)S(1)}, s32[1,256]{1,0:T(1,128)}, u32[]{:S(2)}) copy-start(s32[1,256]{1,0:T(1,128)} %param.12) | copy-start | bytes 3076
  19.2 30.7 %copy-start.3 = (s32[1,256]{1,0:T(1,128)S(1)}, s32[1,256]{1,0:T(1,128)}, u32[]{:S(2)}) copy-start(s32[1,256]{1,0:T(1,128)} %param.13) | copy-start | bytes 3076
  19.2 30.7 %all-to-all-start.1 = ((bf16[16,2,128,256]{3,2,1,0:T(8,128)(2,1)}), bf16[16,2,128,256]{3,2,1,0:T(8,128)(2,1)S(1)}, u32[]{:S(2)}, u32[]{:S(2)}) async-start(bf16[16,2,128,256]{3,2,1,0:T(8,128)(2,1)} %pick.1), calls=%async_computation.1 | async-start | bytes 4194304 | tf_op jit(solution)/shard_map/all_to_all | solution.py:204
  70.5 45.3 %all-to-all-start.2 = ((s16[16,336,256]{2,1,0:T(8,128)(2,1)}), s16[16,336,256]{2,1,0:T(8,128)(2,1)S(1)}, u32[]{:S(2)}, u32[]{:S(2)}) async-start(s16[16,336,256]{2,1,0:T(8,128)(2,1)} %pairs.1), calls=%async_computation.2 | async-start | bytes 5505024 | tf_op jit(solution)/shard_map/all_to_all | solution.py:230
  118.3 4.2 %collective-permute-start = (f32[4,128,256]{2,1,0:T(8,128)S(1)}, f32[4,128,256]{2,1,0:T(8,128)S(1)}, u32[]{:S(2)}, u32[]{:S(2)}) collective-permute-start(f32[4,128,256]{2,1,0:T(8,128)S(1)} %get-tuple-element.8), channel_id=1, source_target_pairs={{0,16},{16,0},{32,48},{48,32},{64,80},{80,64},{96,112},{112,96},{1... | collective-permute-start | bytes 1572872 | tf_op jit(solution)/shard_map/ppermute | solution.py:249
  122.7 15.1 %collective-permute-start.3 = (s16[4,144,256]{2,1,0:T(8,128)(2,1)S(1)}, s16[4,144,256]{2,1,0:T(8,128)(2,1)S(1)}, u32[]{:S(2)}, u32[]{:S(2)}) collective-permute-start(s16[4,144,256]{2,1,0:T(8,128)(2,1)S(1)} %chip.1.own), channel_id=1, source_target_pairs={{0,96},{16,112},{32,0},{48,16},{64,32},{80,48},{96,64},{112,80},{1... | collective-permute-start | bytes 884744 | tf_op jit(solution)/shard_map/ppermute | solution.py:260
  125.6 12.2 %collective-permute-start.2 = (s16[4,144,256]{2,1,0:T(8,128)(2,1)S(1)}, s16[4,144,256]{2,1,0:T(8,128)(2,1)S(1)}, u32[]{:S(2)}, u32[]{:S(2)}) collective-permute-start(s16[4,144,256]{2,1,0:T(8,128)(2,1)S(1)} %chip.1.own), channel_id=1, source_target_pairs={{0,64},{16,80},{32,96},{48,112},{64,0},{80,16},{96,32},{112,48},{1... | collective-permute-start | bytes 884744 | tf_op jit(solution)/shard_map/ppermute | solution.py:260
  125.9 16.4 %collective-permute-start.1 = (s16[4,144,256]{2,1,0:T(8,128)(2,1)S(1)}, s16[4,144,256]{2,1,0:T(8,128)(2,1)S(1)}, u32[]{:S(2)}, u32[]{:S(2)}) collective-permute-start(s16[4,144,256]{2,1,0:T(8,128)(2,1)S(1)} %chip.1.own), channel_id=1, source_target_pairs={{0,32},{16,48},{32,64},{48,80},{64,96},{80,112},{96,0},{112,16},{1... | collective-permute-start | bytes 884744 | tf_op jit(solution)/shard_map/ppermute | solution.py:260
  126.6 17.3 %all-to-all-start.3 = ((s16[16,80,256]{2,1,0:T(8,128)(2,1)}), s16[16,80,256]{2,1,0:T(8,128)(2,1)S(1)}, u32[]{:S(2)}, u32[]{:S(2)}) async-start(s16[16,80,256]{2,1,0:T(8,128)(2,1)} %get-tuple-element.10), calls=%async_computation.3 | async-start | bytes 1310720 | tf_op jit(solution)/shard_map/all_to_all | solution.py:263
  143.3 2.1 %collective-permute-start.4 = (f32[4,128,256]{2,1,0:T(8,128)S(1)}, f32[4,128,256]{2,1,0:T(8,128)S(1)}, u32[]{:S(2)}, u32[]{:S(2)}) collective-permute-start(f32[4,128,256]{2,1,0:T(8,128)S(1)} %ring.1.mine), channel_id=1, source_target_pairs={{0,16},{16,0},{32,48},{48,32},{64,80},{80,64},{96,112},{112,96},{1... | collective-permute-start | bytes 1572872 | tf_op jit(solution)/shard_map/ppermute | solution.py:273

commit v4 on v3

--- a/solution.py
+++ b/solution.py
@@ -1,3 +1,5 @@
+import functools
+
 import jax
 import jax.numpy as jnp
 from jax import lax
@@ -34,6 +36,10 @@
     return pltpu.VMEM(shape, dtype)
 
 
+def hbm():
+    return pl.BlockSpec(memory_space=pl.ANY)
+
+
 def smem():
     return pl.BlockSpec(memory_space=pltpu.SMEM)
 
@@ -63,13 +69,18 @@
     return lax.dot_general(x, y, (((i,), (j,)), ((), ())), preferred_element_type=F32)
 
 
-def pick_kernel(ids, blocks, out):
+def pick_kernel(ids, blocks, out, sems):
+    copies = []
     for i in range(out.shape[0]):
         for q in range(out.shape[1]):
-            out[i, q] = blocks[jnp.maximum(ids[i, q], 0)]
-
-
-def pair_kernel(pu, ps, wanted, conf, rate, users, slots, msg, ugrad, sgrad):
+            block = jnp.maximum(ids[i, q], 0)
+            copies.append(pltpu.make_async_copy(blocks.at[block], out.at[i, q], sems.at[i, q]))
+            copies[-1].start()
+    for copy in copies:
+        copy.wait()
+
+
+def pair_kernel(pu, ps, conf, rate, users, slots, out, ugrad, sgrad, msg, sems):
     step = pl.program_id(0)
     count = conf.shape[0]
     tile = conf.shape[1]
@@ -102,6 +113,7 @@
         cap = sgrad.shape[0] // owners
         part = (msg.shape[1] - META) - cap * tile
         per = tile // part
+        copies = []
         for i in range(owners):
             rows = []
             for q in range(cap):
@@ -113,16 +125,19 @@
             msg[i, cap * tile : cap * tile + part] = codes
             rows.append(expo)
             msg[i, cap * tile + part :] = meta_rows(rows)
-
-
-def owner_kernel(place, ids, got, keep, give, umsg, acc):
+            copies.append(pltpu.make_async_copy(msg.at[i], out.at[i], sems.at[i]))
+            copies[-1].start()
+        for copy in copies:
+            copy.wait()
+
+
+def item_kernel(place, ids, got, keep, give, acc):
     owners = got.shape[0]
     held, tile, width = acc.shape
     half = held // 2
     cap = ids.shape[1]
     part = (got.shape[1] - META) - cap * tile
     acc[...] = jnp.zeros_like(acc)
-    total = jnp.zeros((part, width), F32)
     for i in range(owners):
         meta = got[i, cap * tile + part :].astype(I32)
         for q in range(cap):
@@ -133,11 +148,20 @@
             def _():
                 acc[block] += value
 
-        total += decode(got[i, cap * tile : cap * tile + part], meta[cap : cap + 1])
     core = place[0]
     for r in range(half):
         keep[r] = acc[core * half + r]
         give[r] = acc[(1 - core) * half + r]
+
+
+def user_kernel(cap, got, umsg):
+    owners, rows, width = umsg.shape
+    part = rows - META
+    first = got.shape[1] - META - part
+    total = jnp.zeros((part, width), F32)
+    for i in range(owners):
+        meta = got[i, first + part :].astype(I32)
+        total += decode(got[i, first : first + part], meta[cap : cap + 1])
     codes, expo = encode(total)
     meta = meta_rows([expo])
     for i in range(owners):
@@ -146,11 +170,13 @@
 
 
 def chip_kernel(keep, got, msg):
-    tile = keep.shape[1]
-    for r in range(keep.shape[0]):
+    half, tile, _ = keep.shape
+    rows = []
+    for r in range(half):
         codes, expo = encode(keep[r] + got[r])
-        msg[r, :tile] = codes
-        msg[r, tile:] = meta_rows([expo])
+        msg[r * tile : (r + 1) * tile] = codes
+        rows.append(expo)
+    msg[half * tile :] = meta_rows(rows)
 
 
 def ring_kernel(place, own, one, two, three, out, stack):
@@ -158,8 +184,8 @@
     chips = stack.shape[0]
     for r in range(half):
         for k, ref in enumerate((own, one, two, three)):
-            meta = ref[r, tile:].astype(I32)
-            stack[k] = decode(ref[r, :tile], meta[0:1])
+            meta = ref[half * tile :].astype(I32)
+            stack[k] = decode(ref[r * tile : (r + 1) * tile], meta[r : r + 1])
         total = stack[lax.rem(place[1], chips)]
         for y in range(1, chips):
             total += stack[lax.rem(place[1] + chips - y, chips)]
@@ -196,11 +222,12 @@
     outgoing = pl.pallas_call(
         pick_kernel,
         out_shape=pltpu.HBM((owners, cap, tile, width), item_factors.dtype),
-        in_specs=[smem(), vmem()],
-        out_specs=vmem(),
+        in_specs=[smem(), hbm()],
+        out_specs=hbm(),
+        scratch_shapes=[pltpu.SemaphoreType.DMA((owners, cap))],
         compiler_params=params(),
         name="pick",
-    )(asked, item_factors)
+    )(asked, far(item_factors))
     incoming = lax.all_to_all(outgoing, "items", 0, 0, tiled=True)
     slots = near(incoming.reshape(owners * cap, tile, width))
 
@@ -209,7 +236,7 @@
         pair_kernel,
         out_shape=pltpu.HBM((owners, depth, width), I16),
         grid_spec=pltpu.PrefetchScalarGridSpec(
-            num_scalar_prefetch=3,
+            num_scalar_prefetch=2,
             grid=(count // step,),
             in_specs=[
                 pl.BlockSpec((step, tile, tile), lambda p, *_: (p, 0, 0)),
@@ -217,45 +244,52 @@
                 vmem(),
                 vmem(),
             ],
-            out_specs=vmem(),
+            out_specs=hbm(),
             scratch_shapes=[
                 pltpu.VMEM(user_factors.shape, F32),
                 pltpu.VMEM((owners * cap, tile, width), F32),
+                pltpu.VMEM((owners, depth, width), I16),
+                pltpu.SemaphoreType.DMA((owners,)),
             ],
         ),
         compiler_params=params(),
         name="pairs",
-    )(pair_user[0], pair_slot[0], wanted, far(confidence[0]), far(ratings[0]), user_factors, slots)
+    )(pair_user[0], pair_slot[0], far(confidence[0]), far(ratings[0]), user_factors, slots)
 
     back = lax.all_to_all(msg, "items", 0, 0, tiled=True)
     half = (held // 2, tile, width)
     row = lax.axis_index("users")
     place = jnp.stack([row % 2, row // 2]).astype(I32)
-    keep, give, umsg = pl.pallas_call(
-        owner_kernel,
-        out_shape=(
-            made(half, F32),
-            made(half, F32),
-            pltpu.HBM((owners, part + META, width), I16),
-        ),
+    keep, give = pl.pallas_call(
+        item_kernel,
+        out_shape=(made(half, F32), made(half, F32)),
         in_specs=[smem(), smem(), vmem()],
-        out_specs=(vmem(), vmem(), vmem()),
+        out_specs=(vmem(), vmem()),
         scratch_shapes=[pltpu.VMEM(item_factors.shape, F32)],
         compiler_params=params(),
         name="owners",
     )(place, asked, near(back))
 
     swap = [(u, u ^ 1) for u in range(rows)]
+    back, give = lax.optimization_barrier((back, give))
     mate = lax.ppermute(give, "users", swap)
+    umsg = pl.pallas_call(
+        functools.partial(user_kernel, cap),
+        out_shape=pltpu.HBM((owners, part + META, width), I16),
+        in_specs=[vmem()],
+        out_specs=vmem(),
+        compiler_params=params(),
+        name="users",
+    )(near(back))
+    keep, umsg = lax.optimization_barrier((keep, umsg))
     code = pl.pallas_call(
         chip_kernel,
-        out_shape=made((held // 2, tile + META, width), I16),
+        out_shape=made((held // 2 * tile + META, width), I16),
         in_specs=[vmem(), vmem()],
         out_specs=vmem(),
         compiler_params=params(),
         name="chip",
     )(near(keep), near(mate))
-    code, umsg = lax.optimization_barrier((code, umsg))
     ring = [
         lax.ppermute(code, "users", [(u, (u + 2 * k) % rows) for u in range(rows)])
         for k in range(1, 4)

time: 147 us -> 203 us (1.38)
  Pallas kernels: 29 us -> 92.1 us
  waiting for transfers between devices: 79.3 us -> 46 us
  blocking collectives: 14.6 us -> 45.6 us
  starting transfers between devices: 21.4 us -> 17.1 us
    pallas_call x1, Pallas kernels: 2.14 us -> 65.6 us  [body(): pl.pallas_call(pick_kernel, out_shape=pltpu.HBM((owners, cap, tile, width...]
    all_to_all x0 -> x1, blocking collectives: none -> 31 us  [body(): incoming = lax.all_to_all(outgoing, 'items', 0, 0, tiled=True)]
    all_to_all x1 -> x0, waiting for transfers between devices: 26.7 us -> none  [body(): incoming = lax.all_to_all(outgoing, 'items', 0, 0, tiled=True)]
    all_to_all x1, waiting for transfers between devices: 38.4 us -> 34.1 us  [body(): back = lax.all_to_all(msg, 'items', 0, 0, tiled=True)]
    all_to_all x1 -> x0, starting transfers between devices: 3.86 us -> none  [body(): incoming = lax.all_to_all(outgoing, 'items', 0, 0, tiled=True)]
    all_to_all x1, starting transfers between devices: 6.8 us -> 3.74 us  [body(): back = lax.all_to_all(msg, 'items', 0, 0, tiled=True)]
    ppermute x1, starting transfers between devices: 2.7 us -> 5.32 us  [body(): mate = lax.ppermute(give, 'users', swap)]
  transfers between devices with their start and end apart: 8 -> 7, of which waited for: 6 -> 5; matrix products, arithmetic and copies ran while one was open for 0% -> 0% of each run, Pallas kernels for 1% -> 2%
where the time goes in v4:
time: 203 us; the launch traced here: 202 us
  Pallas kernels  92.1 us (45%)
  waiting for transfers between devices  46 us (23%)
  blocking collectives  45.6 us (22%)
  starting transfers between devices  17.1 us (8%)
    pallas_call x1, Pallas kernels, body(): pl.pallas_call(pick_kernel, out_shape=pltpu.HBM((owners, cap, tile, width...  65.6 us
    all_to_all x1, waiting for transfers between devices, body(): back = lax.all_to_all(msg, 'items', 0, 0, tiled=True)  34.1 us
    all_to_all x1, blocking collectives, body(): incoming = lax.all_to_all(outgoing, 'items', 0, 0, tiled=True)  31 us
    pallas_call x1, Pallas kernels, body(): pl.pallas_call(pair_kernel, out_shape=pltpu.HBM((owners, depth, width), I...  20.2 us
    all_to_all x1, blocking collectives, body(): asked = lax.all_to_all(wanted, 'items', 0, 0, tiled=True)  14.6 us
    ppermute x3, waiting for transfers between devices, body(): lax.ppermute(code, 'users', [(u, (u + 2 * k) % rows) for u in range(rows)])  11 us
    ppermute x1, starting transfers between devices, body(): mate = lax.ppermute(give, 'users', swap)  5.32 us
  transfers between devices with their start and end apart: 7, of which 5 were waited for; matrix products, arithmetic and copies ran while one was open for 0% of the time, Pallas kernels for 2%

profile of v4, /device:TPU:1, one launch (start us, length us, event | category | flops | bytes accessed | tf_op | source)
XLA Modules:
  0.0 202.4 jit_solution(13104548092600840097)
XLA Ops:
  0.6 0.8 copy.11
  1.4 14.6 %all_to_all.26 = s32[16,1,2]{2,1,0:T(1,128)S(1)} all-to-all(s32[16,1,2]{2,1,0:T(1,128)S(1)} %copy.11), channel_id=1, replica_groups=mesh['users'=8,'items'=16] {'items'}, dimensions={0} | all-to-all | bytes 256 | tf_op jit(solution)/shard_map/all_to_all | solution.py:221
  16.0 65.6 %pick.1 = bf16[16,2,128,256]{3,2,1,0:T(8,128)(2,1)} custom-call(s32[16,2]{1,0:T(8,128)S(1)} %bitcast.10, bf16[8,128,256]{2,1,0:T(8,128)(2,1)} %blocks.1), custom_call_target="tpu_custom_call" | custom-call | tf_op jit(solution)/shard_map/pick/pallas_call | solution.py:222
  81.6 0.0 copy-start
  81.6 0.0 copy-start.1
  81.6 0.0 copy-start.2
  81.6 31.0 %all_to_all.27 = bf16[16,2,128,256]{3,2,1,0:T(8,128)(2,1)S(1)} all-to-all(bf16[16,2,128,256]{3,2,1,0:T(8,128)(2,1)} %pick.1), channel_id=1, replica_groups=mesh['users'=8,'items'=16] {'items'}, dimensions={0} | all-to-all | bytes 4194304 | tf_op jit(solution)/shard_map/all_to_all | solution.py:231
  112.6 0.0 copy-done
  112.6 0.0 copy-done.1
  112.7 0.0 copy-done.2
  112.7 20.2 %pairs.1 = s16[16,336,256]{2,1,0:T(8,128)(2,1)} custom-call(s32[256]{0:T(256)S(1)} %bitcast.12, s32[256]{0:T(256)S(1)} %bitcast.13, bf16[256,128,128]{2,1,0:T(8,128)(2,1)} %bitcast.14, bf16[256,128,128]{2,1,0:T(8,128)(2,1)} %bitcast.15, bf16[8,128,256]{2,1,0:T(8,128)(2,1)S(1)} %copy-done, bf16[32,128,256]{2,1,0:T(8,128)(2,1)S(1)} %bitcast.9), custom_call_target="tpu_custom_call" | custom-call | tf_op jit(solution)/shard_map/pairs/pallas_call | solution.py:235
  132.9 3.7 %all-to-all-start.2 = ((s16[16,336,256]{2,1,0:T(8,128)(2,1)}), s16[16,336,256]{2,1,0:T(8,128)(2,1)S(1)}, u32[]{:S(2)}, u32[]{:S(2)}) async-start(s16[16,336,256]{2,1,0:T(8,128)(2,1)} %pairs.1), calls=%async_computation.2 | async-start | bytes 5505024 | tf_op jit(solution)/shard_map/all_to_all | solution.py:259
  136.7 0.1 pad_add_fusion.place
  136.8 34.1 %all-to-all-done.2.got = s16[16,336,256]{2,1,0:T(8,128)(2,1)S(1)} async-done(((s16[16,336,256]{2,1,0:T(8,128)(2,1)}), s16[16,336,256]{2,1,0:T(8,128)(2,1)S(1)}, u32[]{:S(2)}, u32[]{:S(2)}) %all-to-all-start.2) | async-done | bytes 2752544 | tf_op jit(solution)/shard_map/all_to_all | solution.py:259
  170.8 1.5 owners.1
  172.3 5.3 %collective-permute-start = (f32[4,128,256]{2,1,0:T(8,128)S(1)}, f32[4,128,256]{2,1,0:T(8,128)S(1)}, u32[]{:S(2)}, u32[]{:S(2)}) collective-permute-start(f32[4,128,256]{2,1,0:T(8,128)S(1)} %get-tuple-element.13), channel_id=1, source_target_pairs={{0,16},{16,0},{32,48},{48,32},{64,80},{80,64},{96,112},{112,96},{1... | collective-permute-start | bytes 1572872 | tf_op jit(solution)/shard_map/ppermute | solution.py:275
  177.7 1.1 users.3
  178.7 0.5 collective-permute-done.got
  179.2 0.1 chip.1.own
  179.3 2.7 %collective-permute-start.3 = (s16[528,256]{1,0:T(8,128)(2,1)S(1)}, s16[528,256]{1,0:T(8,128)(2,1)S(1)}, u32[]{:S(2)}, u32[]{:S(2)}) collective-permute-start(s16[528,256]{1,0:T(8,128)(2,1)S(1)} %chip.1.own), channel_id=1, source_target_pairs={{0,96},{16,112},{32,0},{48,16},{64,32},{80,48},{96,64},{112,80},{1... | collective-permute-start | bytes 811016 | tf_op jit(solution)/shard_map/ppermute | solution.py:294
  182.1 0.5 collective-permute-start.2
  182.5 0.6 collective-permute-start.1
  183.2 3.6 %all-to-all-start.3 = ((s16[16,80,256]{2,1,0:T(8,128)(2,1)}), s16[16,80,256]{2,1,0:T(8,128)(2,1)S(1)}, u32[]{:S(2)}, u32[]{:S(2)}) async-start(s16[16,80,256]{2,1,0:T(8,128)(2,1)} %users.3), calls=%async_computation.3 | async-start | bytes 1310720 | tf_op jit(solution)/shard_map/all_to_all | solution.py:297
  186.8 6.4 %collective-permute-done.3.three = s16[528,256]{1,0:T(8,128)(2,1)S(1)} collective-permute-done((s16[528,256]{1,0:T(8,128)(2,1)S(1)}, s16[528,256]{1,0:T(8,128)(2,1)S(1)}, u32[]{:S(2)}, u32[]{:S(2)}) %collective-permute-start.3) | collective-permute-done | bytes 270368 | tf_op jit(solution)/shard_map/ppermute | solution.py:294
  193.2 0.0 collective-permute-done.2.two
  193.2 4.6 %collective-permute-done.1.one = s16[528,256]{1,0:T(8,128)(2,1)S(1)} collective-permute-done((s16[528,256]{1,0:T(8,128)(2,1)S(1)}, s16[528,256]{1,0:T(8,128)(2,1)S(1)}, u32[]{:S(2)}, u32[]{:S(2)}) %collective-permute-start.1) | collective-permute-done | bytes 270368 | tf_op jit(solution)/shard_map/ppermute | solution.py:294
  197.8 0.9 ring.1.mine
  198.7 0.6 collective-permute-start.4
  199.3 0.0 all-to-all-done.3.got
  199.3 1.1 spread.1
  200.4 0.4 collective-permute-done.4.other
  200.8 1.6 join.1
Async XLA Ops:
  81.6 31.0 %copy-start = (bf16[8,128,256]{2,1,0:T(8,128)(2,1)S(1)}, bf16[8,128,256]{2,1,0:T(8,128)(2,1)}, u32[]{:S(2)}) copy-start(bf16[8,128,256]{2,1,0:T(8,128)(2,1)} %users.2) | copy-start | bytes 1572868
  81.6 31.0 %copy-start.1 = (s32[1,256]{1,0:T(1,128)S(1)}, s32[1,256]{1,0:T(1,128)}, u32[]{:S(2)}) copy-start(s32[1,256]{1,0:T(1,128)} %param.12) | copy-start | bytes 3076
  81.6 31.0 %copy-start.2 = (s32[1,256]{1,0:T(1,128)S(1)}, s32[1,256]{1,0:T(1,128)}, u32[]{:S(2)}) copy-start(s32[1,256]{1,0:T(1,128)} %param.13) | copy-start | bytes 3076
  132.9 37.9 %all-to-all-start.2 = ((s16[16,336,256]{2,1,0:T(8,128)(2,1)}), s16[16,336,256]{2,1,0:T(8,128)(2,1)S(1)}, u32[]{:S(2)}, u32[]{:S(2)}) async-start(s16[16,336,256]{2,1,0:T(8,128)(2,1)} %pairs.1), calls=%async_computation.2 | async-start | bytes 5505024 | tf_op jit(solution)/shard_map/all_to_all | solution.py:259
  172.3 6.9 %collective-permute-start = (f32[4,128,256]{2,1,0:T(8,128)S(1)}, f32[4,128,256]{2,1,0:T(8,128)S(1)}, u32[]{:S(2)}, u32[]{:S(2)}) collective-permute-start(f32[4,128,256]{2,1,0:T(8,128)S(1)} %get-tuple-element.13), channel_id=1, source_target_pairs={{0,16},{16,0},{32,48},{48,32},{64,80},{80,64},{96,112},{112,96},{1... | collective-permute-start | bytes 1572872 | tf_op jit(solution)/shard_map/ppermute | solution.py:275
  179.3 13.9 %collective-permute-start.3 = (s16[528,256]{1,0:T(8,128)(2,1)S(1)}, s16[528,256]{1,0:T(8,128)(2,1)S(1)}, u32[]{:S(2)}, u32[]{:S(2)}) collective-permute-start(s16[528,256]{1,0:T(8,128)(2,1)S(1)} %chip.1.own), channel_id=1, source_target_pairs={{0,96},{16,112},{32,0},{48,16},{64,32},{80,48},{96,64},{112,80},{1... | collective-permute-start | bytes 811016 | tf_op jit(solution)/shard_map/ppermute | solution.py:294
  182.1 11.1 %collective-permute-start.2 = (s16[528,256]{1,0:T(8,128)(2,1)S(1)}, s16[528,256]{1,0:T(8,128)(2,1)S(1)}, u32[]{:S(2)}, u32[]{:S(2)}) collective-permute-start(s16[528,256]{1,0:T(8,128)(2,1)S(1)} %chip.1.own), channel_id=1, source_target_pairs={{0,64},{16,80},{32,96},{48,112},{64,0},{80,16},{96,32},{112,48},{1... | collective-permute-start | bytes 811016 | tf_op jit(solution)/shard_map/ppermute | solution.py:294
  182.5 15.2 %collective-permute-start.1 = (s16[528,256]{1,0:T(8,128)(2,1)S(1)}, s16[528,256]{1,0:T(8,128)(2,1)S(1)}, u32[]{:S(2)}, u32[]{:S(2)}) collective-permute-start(s16[528,256]{1,0:T(8,128)(2,1)S(1)} %chip.1.own), channel_id=1, source_target_pairs={{0,32},{16,48},{32,64},{48,80},{64,96},{80,112},{96,0},{112,16},{1... | collective-permute-start | bytes 811016 | tf_op jit(solution)/shard_map/ppermute | solution.py:294
  183.2 16.1 %all-to-all-start.3 = ((s16[16,80,256]{2,1,0:T(8,128)(2,1)}), s16[16,80,256]{2,1,0:T(8,128)(2,1)S(1)}, u32[]{:S(2)}, u32[]{:S(2)}) async-start(s16[16,80,256]{2,1,0:T(8,128)(2,1)} %users.3), calls=%async_computation.3 | async-start | bytes 1310720 | tf_op jit(solution)/shard_map/all_to_all | solution.py:297
  198.7 2.1 %collective-permute-start.4 = (f32[4,128,256]{2,1,0:T(8,128)S(1)}, f32[4,128,256]{2,1,0:T(8,128)S(1)}, u32[]{:S(2)}, u32[]{:S(2)}) collective-permute-start(f32[4,128,256]{2,1,0:T(8,128)S(1)} %ring.1.mine), channel_id=1, source_target_pairs={{0,16},{16,0},{32,48},{48,32},{64,80},{80,64},{96,112},{112,96},{1... | collective-permute-start | bytes 1572872 | tf_op jit(solution)/shard_map/ppermute | solution.py:307

commit v5 on v4

--- a/solution.py
+++ b/solution.py
@@ -36,10 +36,6 @@
     return pltpu.VMEM(shape, dtype)
 
 
-def hbm():
-    return pl.BlockSpec(memory_space=pl.ANY)
-
-
 def smem():
     return pl.BlockSpec(memory_space=pltpu.SMEM)
 
@@ -69,18 +65,13 @@
     return lax.dot_general(x, y, (((i,), (j,)), ((), ())), preferred_element_type=F32)
 
 
-def pick_kernel(ids, blocks, out, sems):
-    copies = []
+def pick_kernel(ids, blocks, out):
     for i in range(out.shape[0]):
         for q in range(out.shape[1]):
-            block = jnp.maximum(ids[i, q], 0)
-            copies.append(pltpu.make_async_copy(blocks.at[block], out.at[i, q], sems.at[i, q]))
-            copies[-1].start()
-    for copy in copies:
-        copy.wait()
-
-
-def pair_kernel(pu, ps, conf, rate, users, slots, out, ugrad, sgrad, msg, sems):
+            out[i, q] = blocks[jnp.maximum(ids[i, q], 0)]
+
+
+def pair_kernel(pu, ps, conf, rate, users, slots, msg, ugrad, sgrad):
     step = pl.program_id(0)
     count = conf.shape[0]
     tile = conf.shape[1]
@@ -113,7 +104,6 @@
         cap = sgrad.shape[0] // owners
         part = (msg.shape[1] - META) - cap * tile
         per = tile // part
-        copies = []
         for i in range(owners):
             rows = []
             for q in range(cap):
@@ -125,10 +115,6 @@
             msg[i, cap * tile : cap * tile + part] = codes
             rows.append(expo)
             msg[i, cap * tile + part :] = meta_rows(rows)
-            copies.append(pltpu.make_async_copy(msg.at[i], out.at[i], sems.at[i]))
-            copies[-1].start()
-        for copy in copies:
-            copy.wait()
 
 
 def item_kernel(place, ids, got, keep, give, acc):
@@ -216,25 +202,26 @@
     count = pair_user.shape[1]
     part = user_factors.shape[0] * tile // owners
     step = min(STEP, count)
-    wanted = slot_blocks[0]
+    row = lax.axis_index("users").astype(I32)
+    place = jnp.stack([row & 1, row >> 1])
+    wanted, place = lax.optimization_barrier((slot_blocks[0], place))
 
     asked = lax.all_to_all(wanted, "items", 0, 0, tiled=True)
     outgoing = pl.pallas_call(
         pick_kernel,
-        out_shape=pltpu.HBM((owners, cap, tile, width), item_factors.dtype),
-        in_specs=[smem(), hbm()],
-        out_specs=hbm(),
-        scratch_shapes=[pltpu.SemaphoreType.DMA((owners, cap))],
+        out_shape=made((owners, cap, tile, width), item_factors.dtype),
+        in_specs=[smem(), vmem()],
+        out_specs=vmem(),
         compiler_params=params(),
         name="pick",
-    )(asked, far(item_factors))
+    )(asked, near(item_factors))
     incoming = lax.all_to_all(outgoing, "items", 0, 0, tiled=True)
     slots = near(incoming.reshape(owners * cap, tile, width))
 
     depth = cap * tile + part + META
     msg = pl.pallas_call(
         pair_kernel,
-        out_shape=pltpu.HBM((owners, depth, width), I16),
+        out_shape=made((owners, depth, width), I16),
         grid_spec=pltpu.PrefetchScalarGridSpec(
             num_scalar_prefetch=2,
             grid=(count // step,),
@@ -244,12 +231,10 @@
                 vmem(),
                 vmem(),
             ],
-            out_specs=hbm(),
+            out_specs=vmem(),
             scratch_shapes=[
                 pltpu.VMEM(user_factors.shape, F32),
                 pltpu.VMEM((owners * cap, tile, width), F32),
-                pltpu.VMEM((owners, depth, width), I16),
-                pltpu.SemaphoreType.DMA((owners,)),
             ],
         ),
         compiler_params=params(),
@@ -258,8 +243,6 @@
 
     back = lax.all_to_all(msg, "items", 0, 0, tiled=True)
     half = (held // 2, tile, width)
-    row = lax.axis_index("users")
-    place = jnp.stack([row % 2, row // 2]).astype(I32)
     keep, give = pl.pallas_call(
         item_kernel,
         out_shape=(made(half, F32), made(half, F32)),

time: 203 us -> 134 us (0.66)
  Pallas kernels: 92.1 us -> 27.3 us
  waiting for transfers between devices: 46 us -> 12 us
  blocking collectives: 45.6 us -> 79 us
  starting transfers between devices: 17.1 us -> 12.6 us
    pallas_call x2, Pallas kernels: 85.8 us -> 21 us  [the longest x1 20.2 us: body(): pl.pallas_call(pair_kernel, out_shape=made((owners, depth, width), I16),...]
    all_to_all x0 -> x1, blocking collectives: none -> 34.5 us  [body(): back = lax.all_to_all(msg, 'items', 0, 0, tiled=True)]
    all_to_all x1 -> x0, waiting for transfers between devices: 34.1 us -> none  [body(): back = lax.all_to_all(msg, 'items', 0, 0, tiled=True)]
    all_to_all x1 -> x0, starting transfers between devices: 3.74 us -> none  [body(): back = lax.all_to_all(msg, 'items', 0, 0, tiled=True)]
  transfers between devices with their start and end apart: 7 -> 6, of which waited for: 5 -> 4; matrix products, arithmetic and copies ran while one was open for 0% -> 0% of each run, Pallas kernels for 2% -> 2%
where the time goes in v5:
time: 134 us
  blocking collectives  79 us (59%)
  Pallas kernels  27.3 us (20%)
  starting transfers between devices  12.6 us (9%)
  waiting for transfers between devices  12 us (9%)
  local copies, waits for them, and re-layouts  1.82 us (1%)
    all_to_all x1, blocking collectives, body(): back = lax.all_to_all(msg, 'items', 0, 0, tiled=True)  34.5 us
    all_to_all x1, blocking collectives, body(): incoming = lax.all_to_all(outgoing, 'items', 0, 0, tiled=True)  30 us
    pallas_call x1, Pallas kernels, body(): pl.pallas_call(pair_kernel, out_shape=made((owners, depth, width), I16),...  20.2 us
    all_to_all x1, blocking collectives, body(): asked = lax.all_to_all(wanted, 'items', 0, 0, tiled=True)  14.6 us
    ppermute x3, waiting for transfers between devices, body(): lax.ppermute(code, 'users', [(u, (u + 2 * k) % rows) for u in range(rows)])  11.1 us
    ppermute x1, starting transfers between devices, body(): mate = lax.ppermute(give, 'users', swap)  4.63 us
    ppermute x3, starting transfers between devices, body(): lax.ppermute(code, 'users', [(u, (u + 2 * k) % rows) for u in range(rows)])  3.83 us
    all_to_all x1, starting transfers between devices, body(): ugot = lax.all_to_all(umsg, 'items', 0, 0, tiled=True)  3.59 us
  transfers between devices with their start and end apart: 6, of which 4 were waited for; matrix products, arithmetic and copies ran while one was open for 0% of the time, Pallas kernels for 2%

profile of v5, /device:TPU:1, one launch (start us, length us, event | category | flops | bytes accessed | tf_op | source)
XLA Modules:
  0.0 133.6 jit_solution(14507199327990498569)
XLA Ops:
  0.6 0.1 pad_add_fusion.place
  0.7 0.8 copy.11
  1.5 14.6 %all_to_all.26 = s32[16,1,2]{2,1,0:T(1,128)S(1)} all-to-all(s32[16,1,2]{2,1,0:T(1,128)S(1)} %copy.11), channel_id=1, replica_groups=mesh['users'=8,'items'=16] {'items'}, dimensions={0} | all-to-all | bytes 256 | tf_op jit(solution)/shard_map/all_to_all | solution.py:209
  16.1 1.0 copy-done
  17.1 0.8 pick.1
  17.9 0.0 copy-start.1
  18.0 0.0 copy-start.2
  18.0 0.0 copy-start.3
  18.0 30.0 %all_to_all.27 = bf16[16,2,128,256]{3,2,1,0:T(8,128)(2,1)S(1)} all-to-all(bf16[16,2,128,256]{3,2,1,0:T(8,128)(2,1)S(1)} %pick.1), channel_id=1, replica_groups=mesh['users'=8,'items'=16] {'items'}, dimensions={0} | all-to-all | bytes 4194304 | tf_op jit(solution)/shard_map/all_to_all | solution.py:218
  48.0 0.0 copy-done.1
  48.0 0.0 copy-done.2
  48.0 0.0 copy-done.3
  48.0 20.2 %pairs.1 = s16[16,336,256]{2,1,0:T(8,128)(2,1)S(1)} custom-call(s32[256]{0:T(256)S(1)} %bitcast.13, s32[256]{0:T(256)S(1)} %bitcast.14, bf16[256,128,128]{2,1,0:T(8,128)(2,1)} %bitcast.15, bf16[256,128,128]{2,1,0:T(8,128)(2,1)} %bitcast.16, bf16[8,128,256]{2,1,0:T(8,128)(2,1)S(1)} %copy-done.1, bf16[32,128,256]{2,1,0:T(8,128)(2,1)S(1)} %bitcast.10), custom_call_target="tpu_custom_call" | custom-call | tf_op jit(solution)/shard_map/pairs/pallas_call | solution.py:222
  68.2 34.5 %all_to_all.28.got = s16[16,336,256]{2,1,0:T(8,128)(2,1)S(1)} all-to-all(s16[16,336,256]{2,1,0:T(8,128)(2,1)S(1)} %pairs.1), channel_id=1, replica_groups=mesh['users'=8,'items'=16] {'items'}, dimensions={0} | all-to-all | bytes 5505024 | tf_op jit(solution)/shard_map/all_to_all | solution.py:244
  102.6 1.5 %owners.1 = (f32[4,128,256]{2,1,0:T(8,128)S(1)}, f32[4,128,256]{2,1,0:T(8,128)S(1)}) custom-call(s32[2]{0:T(128)S(1)} %pad_add_fusion.place, s32[16,2]{1,0:T(8,128)S(1)} %bitcast.12, s16[16,336,256]{2,1,0:T(8,128)(2,1)S(1)} %all_to_all.28.got), custom_call_target="tpu_custom_call" | custom-call | tf_op jit(solution)/shard_map/owners/pallas_call | solution.py:246
  104.1 4.6 %collective-permute-start = (f32[4,128,256]{2,1,0:T(8,128)S(1)}, f32[4,128,256]{2,1,0:T(8,128)S(1)}, u32[]{:S(2)}, u32[]{:S(2)}) collective-permute-start(f32[4,128,256]{2,1,0:T(8,128)S(1)} %get-tuple-element.17), channel_id=1, source_target_pairs={{0,16},{16,0},{32,48},{48,32},{64,80},{80,64},{96,112},{112,96},{1... | collective-permute-start | bytes 1572872 | tf_op jit(solution)/shard_map/ppermute | solution.py:258
  108.7 1.1 users.3
  109.8 0.5 collective-permute-done.got
  110.3 0.1 chip.1.own
  110.4 2.8 %collective-permute-start.3 = (s16[528,256]{1,0:T(8,128)(2,1)S(1)}, s16[528,256]{1,0:T(8,128)(2,1)S(1)}, u32[]{:S(2)}, u32[]{:S(2)}) collective-permute-start(s16[528,256]{1,0:T(8,128)(2,1)S(1)} %chip.1.own), channel_id=1, source_target_pairs={{0,96},{16,112},{32,0},{48,16},{64,32},{80,48},{96,64},{112,80},{1... | collective-permute-start | bytes 811016 | tf_op jit(solution)/shard_map/ppermute | solution.py:277
  113.2 0.3 collective-permute-start.2
  113.6 0.7 collective-permute-start.1
  114.3 3.6 %all-to-all-start.3 = ((s16[16,80,256]{2,1,0:T(8,128)(2,1)}), s16[16,80,256]{2,1,0:T(8,128)(2,1)S(1)}, u32[]{:S(2)}, u32[]{:S(2)}) async-start(s16[16,80,256]{2,1,0:T(8,128)(2,1)} %users.3), calls=%async_computation.3 | async-start | bytes 1310720 | tf_op jit(solution)/shard_map/all_to_all | solution.py:280
  117.9 6.5 %collective-permute-done.3.three = s16[528,256]{1,0:T(8,128)(2,1)S(1)} collective-permute-done((s16[528,256]{1,0:T(8,128)(2,1)S(1)}, s16[528,256]{1,0:T(8,128)(2,1)S(1)}, u32[]{:S(2)}, u32[]{:S(2)}) %collective-permute-start.3) | collective-permute-done | bytes 270368 | tf_op jit(solution)/shard_map/ppermute | solution.py:277
  124.4 0.0 collective-permute-done.2.two
  124.4 4.6 %collective-permute-done.1.one = s16[528,256]{1,0:T(8,128)(2,1)S(1)} collective-permute-done((s16[528,256]{1,0:T(8,128)(2,1)S(1)}, s16[528,256]{1,0:T(8,128)(2,1)S(1)}, u32[]{:S(2)}, u32[]{:S(2)}) %collective-permute-start.1) | collective-permute-done | bytes 270368 | tf_op jit(solution)/shard_map/ppermute | solution.py:277
  128.9 0.9 ring.1.mine
  129.9 0.6 collective-permute-start.4
  130.4 0.0 all-to-all-done.3.got
  130.4 1.1 spread.1
  131.5 0.4 collective-permute-done.4.other
  132.0 1.6 %join.1 = f32[8,128,256]{2,1,0:T(8,128)} custom-call(s32[2]{0:T(128)S(1)} %pad_add_fusion.place, f32[4,128,256]{2,1,0:T(8,128)S(1)} %ring.1.mine, f32[4,128,256]{2,1,0:T(8,128)S(1)} %collective-permute-done.4.other), custom_call_target="tpu_custom_call" | custom-call | tf_op jit(solution)/shard_map/join/pallas_call | solution.py:291
  (1 shorter events, 0.0 us)
Async XLA Ops:
  16.1 1.0 copy-start
  17.9 30.0 %copy-start.1 = (bf16[8,128,256]{2,1,0:T(8,128)(2,1)S(1)}, bf16[8,128,256]{2,1,0:T(8,128)(2,1)}, u32[]{:S(2)}) copy-start(bf16[8,128,256]{2,1,0:T(8,128)(2,1)} %users.2) | copy-start | bytes 1572868
  18.0 30.0 %copy-start.2 = (s32[1,256]{1,0:T(1,128)S(1)}, s32[1,256]{1,0:T(1,128)}, u32[]{:S(2)}) copy-start(s32[1,256]{1,0:T(1,128)} %param.12) | copy-start | bytes 3076
  18.0 30.0 %copy-start.3 = (s32[1,256]{1,0:T(1,128)S(1)}, s32[1,256]{1,0:T(1,128)}, u32[]{:S(2)}) copy-start(s32[1,256]{1,0:T(1,128)} %param.13) | copy-start | bytes 3076
  104.1 6.2 %collective-permute-start = (f32[4,128,256]{2,1,0:T(8,128)S(1)}, f32[4,128,256]{2,1,0:T(8,128)S(1)}, u32[]{:S(2)}, u32[]{:S(2)}) collective-permute-start(f32[4,128,256]{2,1,0:T(8,128)S(1)} %get-tuple-element.17), channel_id=1, source_target_pairs={{0,16},{16,0},{32,48},{48,32},{64,80},{80,64},{96,112},{112,96},{1... | collective-permute-start | bytes 1572872 | tf_op jit(solution)/shard_map/ppermute | solution.py:258
  110.4 14.0 %collective-permute-start.3 = (s16[528,256]{1,0:T(8,128)(2,1)S(1)}, s16[528,256]{1,0:T(8,128)(2,1)S(1)}, u32[]{:S(2)}, u32[]{:S(2)}) collective-permute-start(s16[528,256]{1,0:T(8,128)(2,1)S(1)} %chip.1.own), channel_id=1, source_target_pairs={{0,96},{16,112},{32,0},{48,16},{64,32},{80,48},{96,64},{112,80},{1... | collective-permute-start | bytes 811016 | tf_op jit(solution)/shard_map/ppermute | solution.py:277
  113.2 11.1 %collective-permute-start.2 = (s16[528,256]{1,0:T(8,128)(2,1)S(1)}, s16[528,256]{1,0:T(8,128)(2,1)S(1)}, u32[]{:S(2)}, u32[]{:S(2)}) collective-permute-start(s16[528,256]{1,0:T(8,128)(2,1)S(1)} %chip.1.own), channel_id=1, source_target_pairs={{0,64},{16,80},{32,96},{48,112},{64,0},{80,16},{96,32},{112,48},{1... | collective-permute-start | bytes 811016 | tf_op jit(solution)/shard_map/ppermute | solution.py:277
  113.6 15.4 %collective-permute-start.1 = (s16[528,256]{1,0:T(8,128)(2,1)S(1)}, s16[528,256]{1,0:T(8,128)(2,1)S(1)}, u32[]{:S(2)}, u32[]{:S(2)}) collective-permute-start(s16[528,256]{1,0:T(8,128)(2,1)S(1)} %chip.1.own), channel_id=1, source_target_pairs={{0,32},{16,48},{32,64},{48,80},{64,96},{80,112},{96,0},{112,16},{1... | collective-permute-start | bytes 811016 | tf_op jit(solution)/shard_map/ppermute | solution.py:277
  114.3 16.2 %all-to-all-start.3 = ((s16[16,80,256]{2,1,0:T(8,128)(2,1)}), s16[16,80,256]{2,1,0:T(8,128)(2,1)S(1)}, u32[]{:S(2)}, u32[]{:S(2)}) async-start(s16[16,80,256]{2,1,0:T(8,128)(2,1)} %users.3), calls=%async_computation.3 | async-start | bytes 1310720 | tf_op jit(solution)/shard_map/all_to_all | solution.py:280
  129.9 2.1 %collective-permute-start.4 = (f32[4,128,256]{2,1,0:T(8,128)S(1)}, f32[4,128,256]{2,1,0:T(8,128)S(1)}, u32[]{:S(2)}, u32[]{:S(2)}) collective-permute-start(f32[4,128,256]{2,1,0:T(8,128)S(1)} %ring.1.mine), channel_id=1, source_target_pairs={{0,16},{16,0},{32,48},{48,32},{64,80},{80,64},{96,112},{112,96},{1... | collective-permute-start | bytes 1572872 | tf_op jit(solution)/shard_map/ppermute | solution.py:290

commit v6 on v5

--- a/solution.py
+++ b/solution.py
@@ -44,8 +44,7 @@
     top = jnp.max(jnp.abs(x), axis=0, keepdims=True)
     expo = jnp.ceil(jnp.log2(jnp.maximum(top, 1e-30)) + 1e-4)
     scaled = x * jnp.exp2(14.99 - expo)
-    codes = jnp.clip(jnp.round(scaled), -32767.0, 32767.0)
-    return codes.astype(I32).astype(I16), expo.astype(I32)
+    return jnp.round(scaled).astype(I32).astype(I16), expo.astype(I32)
 
 
 def decode(codes, expo):
@@ -178,12 +177,17 @@
         out[r] = total
 
 
-def join_kernel(place, mine, other, out):
+def join_kernel(place, mine, other, out, sems):
     half = mine.shape[0]
     core = place[0]
-    for r in range(half):
-        out[core * half + r] = mine[r]
-        out[(1 - core) * half + r] = other[r]
+    copies = [
+        pltpu.make_async_copy(mine, out.at[pl.ds(core * half, half)], sems.at[0]),
+        pltpu.make_async_copy(other, out.at[pl.ds((1 - core) * half, half)], sems.at[1]),
+    ]
+    for copy in copies:
+        copy.start()
+    for copy in copies:
+        copy.wait()
 
 
 def spread_kernel(got, out):
@@ -258,7 +262,7 @@
     mate = lax.ppermute(give, "users", swap)
     umsg = pl.pallas_call(
         functools.partial(user_kernel, cap),
-        out_shape=pltpu.HBM((owners, part + META, width), I16),
+        out_shape=made((owners, part + META, width), I16),
         in_specs=[vmem()],
         out_specs=vmem(),
         compiler_params=params(),
@@ -273,6 +277,7 @@
         compiler_params=params(),
         name="chip",
     )(near(keep), near(mate))
+    code, umsg = lax.optimization_barrier((code, umsg))
     ring = [
         lax.ppermute(code, "users", [(u, (u + 2 * k) % rows) for u in range(rows)])
         for k in range(1, 4)
@@ -290,9 +295,10 @@
     other = lax.ppermute(mine, "users", swap)
     item_total = pl.pallas_call(
         join_kernel,
-        out_shape=jax.ShapeDtypeStruct(item_factors.shape, F32),
+        out_shape=pltpu.HBM(item_factors.shape, F32),
         in_specs=[smem(), vmem(), vmem()],
-        out_specs=vmem(),
+        out_specs=pl.BlockSpec(memory_space=pl.ANY),
+        scratch_shapes=[pltpu.SemaphoreType.DMA((2,))],
         compiler_params=params(),
         name="join",
     )(place, near(mine), near(other))

time: 134 us -> 134 us (level)
  no operation moved by 1% of the time
where the time goes in v6:
time: 134 us; the launch traced here: 133 us
  blocking collectives  79 us (59%)
  Pallas kernels  27 us (20%)
  starting transfers between devices  12.7 us (9%)
  waiting for transfers between devices  12 us (9%)
  local copies, waits for them, and re-layouts  1.82 us (1%)
    all_to_all x1, blocking collectives, body(): back = lax.all_to_all(msg, 'items', 0, 0, tiled=True)  34.5 us
    all_to_all x1, blocking collectives, body(): incoming = lax.all_to_all(outgoing, 'items', 0, 0, tiled=True)  30 us
    pallas_call x1, Pallas kernels, body(): pl.pallas_call(pair_kernel, out_shape=made((owners, depth, width), I16),...  20 us
    all_to_all x1, blocking collectives, body(): asked = lax.all_to_all(wanted, 'items', 0, 0, tiled=True)  14.6 us
    ppermute x3, waiting for transfers between devices, body(): lax.ppermute(code, 'users', [(u, (u + 2 * k) % rows) for u in range(rows)])  11 us
    ppermute x1, starting transfers between devices, body(): mate = lax.ppermute(give, 'users', swap)  4.69 us
    ppermute x3, starting transfers between devices, body(): lax.ppermute(code, 'users', [(u, (u + 2 * k) % rows) for u in range(rows)])  3.86 us
    all_to_all x1, starting transfers between devices, body(): ugot = lax.all_to_all(umsg, 'items', 0, 0, tiled=True)  3.59 us
  transfers between devices with their start and end apart: 6, of which 4 were waited for; matrix products, arithmetic and copies ran while one was open for 0% of the time, Pallas kernels for 2%

profile of v6, /device:TPU:1, one launch (start us, length us, event | category | flops | bytes accessed | tf_op | source)
XLA Modules:
  0.0 133.3 jit_solution(7186125496621615201)
XLA Ops:
  0.6 0.1 pad_add_fusion.place
  0.7 0.8 copy.11
  1.5 14.6 %all_to_all.26 = s32[16,1,2]{2,1,0:T(1,128)S(1)} all-to-all(s32[16,1,2]{2,1,0:T(1,128)S(1)} %copy.11), channel_id=1, replica_groups=mesh['users'=8,'items'=16] {'items'}, dimensions={0} | all-to-all | bytes 256 | tf_op jit(solution)/shard_map/all_to_all | solution.py:213
  16.1 1.0 copy-done
  17.1 0.8 pick.1
  17.9 0.0 copy-start.1
  18.0 0.0 copy-start.2
  18.0 0.0 copy-start.3
  18.0 30.0 %all_to_all.27 = bf16[16,2,128,256]{3,2,1,0:T(8,128)(2,1)S(1)} all-to-all(bf16[16,2,128,256]{3,2,1,0:T(8,128)(2,1)S(1)} %pick.1), channel_id=1, replica_groups=mesh['users'=8,'items'=16] {'items'}, dimensions={0} | all-to-all | bytes 4194304 | tf_op jit(solution)/shard_map/all_to_all | solution.py:222
  48.0 0.0 copy-done.1
  48.0 0.0 copy-done.2
  48.0 0.0 copy-done.3
  48.0 20.0 %pairs.1 = s16[16,336,256]{2,1,0:T(8,128)(2,1)S(1)} custom-call(s32[256]{0:T(256)S(1)} %bitcast.13, s32[256]{0:T(256)S(1)} %bitcast.14, bf16[256,128,128]{2,1,0:T(8,128)(2,1)} %bitcast.15, bf16[256,128,128]{2,1,0:T(8,128)(2,1)} %bitcast.16, bf16[8,128,256]{2,1,0:T(8,128)(2,1)S(1)} %copy-done.1, bf16[32,128,256]{2,1,0:T(8,128)(2,1)S(1)} %bitcast.10), custom_call_target="tpu_custom_call" | custom-call | tf_op jit(solution)/shard_map/pairs/pallas_call | solution.py:226
  68.0 34.5 %all_to_all.28.got = s16[16,336,256]{2,1,0:T(8,128)(2,1)S(1)} all-to-all(s16[16,336,256]{2,1,0:T(8,128)(2,1)S(1)} %pairs.1), channel_id=1, replica_groups=mesh['users'=8,'items'=16] {'items'}, dimensions={0} | all-to-all | bytes 5505024 | tf_op jit(solution)/shard_map/all_to_all | solution.py:248
  102.4 1.4 %owners.1 = (f32[4,128,256]{2,1,0:T(8,128)S(1)}, f32[4,128,256]{2,1,0:T(8,128)S(1)}) custom-call(s32[2]{0:T(128)S(1)} %pad_add_fusion.place, s32[16,2]{1,0:T(8,128)S(1)} %bitcast.12, s16[16,336,256]{2,1,0:T(8,128)(2,1)S(1)} %all_to_all.28.got), custom_call_target="tpu_custom_call" | custom-call | tf_op jit(solution)/shard_map/owners/pallas_call | solution.py:250
  103.9 4.7 %collective-permute-start = (f32[4,128,256]{2,1,0:T(8,128)S(1)}, f32[4,128,256]{2,1,0:T(8,128)S(1)}, u32[]{:S(2)}, u32[]{:S(2)}) collective-permute-start(f32[4,128,256]{2,1,0:T(8,128)S(1)} %get-tuple-element.18), channel_id=1, source_target_pairs={{0,16},{16,0},{32,48},{48,32},{64,80},{80,64},{96,112},{112,96},{1... | collective-permute-start | bytes 1572872 | tf_op jit(solution)/shard_map/ppermute | solution.py:262
  108.6 1.1 users.3
  109.7 0.5 collective-permute-done.got
  110.1 0.1 chip.1.own
  110.3 2.8 %collective-permute-start.3 = (s16[528,256]{1,0:T(8,128)(2,1)S(1)}, s16[528,256]{1,0:T(8,128)(2,1)S(1)}, u32[]{:S(2)}, u32[]{:S(2)}) collective-permute-start(s16[528,256]{1,0:T(8,128)(2,1)S(1)} %chip.1.own), channel_id=1, source_target_pairs={{0,96},{16,112},{32,0},{48,16},{64,32},{80,48},{96,64},{112,80},{1... | collective-permute-start | bytes 811016 | tf_op jit(solution)/shard_map/ppermute | solution.py:282
  113.1 0.3 collective-permute-start.2
  113.4 0.7 collective-permute-start.1
  114.1 3.6 %all-to-all-start.3 = ((s16[16,80,256]{2,1,0:T(8,128)(2,1)}), s16[16,80,256]{2,1,0:T(8,128)(2,1)S(1)}, u32[]{:S(2)}, u32[]{:S(2)}) async-start(s16[16,80,256]{2,1,0:T(8,128)(2,1)} %users.3), calls=%async_computation.3 | async-start | bytes 1310720 | tf_op jit(solution)/shard_map/all_to_all | solution.py:285
  117.7 6.5 %collective-permute-done.3.three = s16[528,256]{1,0:T(8,128)(2,1)S(1)} collective-permute-done((s16[528,256]{1,0:T(8,128)(2,1)S(1)}, s16[528,256]{1,0:T(8,128)(2,1)S(1)}, u32[]{:S(2)}, u32[]{:S(2)}) %collective-permute-start.3) | collective-permute-done | bytes 270368 | tf_op jit(solution)/shard_map/ppermute | solution.py:282
  124.2 0.0 collective-permute-done.2.two
  124.2 4.6 %collective-permute-done.1.one = s16[528,256]{1,0:T(8,128)(2,1)S(1)} collective-permute-done((s16[528,256]{1,0:T(8,128)(2,1)S(1)}, s16[528,256]{1,0:T(8,128)(2,1)S(1)}, u32[]{:S(2)}, u32[]{:S(2)}) %collective-permute-start.1) | collective-permute-done | bytes 270368 | tf_op jit(solution)/shard_map/ppermute | solution.py:282
  128.8 0.9 ring.1.mine
  129.7 0.6 collective-permute-start.4
  130.3 0.0 all-to-all-done.3.got
  130.3 1.1 spread.1
  131.4 0.4 collective-permute-done.4.other
  131.8 1.5 %join.1 = f32[8,128,256]{2,1,0:T(8,128)} custom-call(s32[2]{0:T(128)S(1)} %pad_add_fusion.place, f32[4,128,256]{2,1,0:T(8,128)S(1)} %ring.1.mine, f32[4,128,256]{2,1,0:T(8,128)S(1)} %collective-permute-done.4.other), custom_call_target="tpu_custom_call" | custom-call | tf_op jit(solution)/shard_map/join/pallas_call | solution.py:296
  (1 shorter events, 0.0 us)
Async XLA Ops:
  16.1 1.0 copy-start
  17.9 30.0 %copy-start.1 = (bf16[8,128,256]{2,1,0:T(8,128)(2,1)S(1)}, bf16[8,128,256]{2,1,0:T(8,128)(2,1)}, u32[]{:S(2)}) copy-start(bf16[8,128,256]{2,1,0:T(8,128)(2,1)} %users.2) | copy-start | bytes 1572868
  18.0 30.0 %copy-start.2 = (s32[1,256]{1,0:T(1,128)S(1)}, s32[1,256]{1,0:T(1,128)}, u32[]{:S(2)}) copy-start(s32[1,256]{1,0:T(1,128)} %param.12) | copy-start | bytes 3076
  18.0 30.0 %copy-start.3 = (s32[1,256]{1,0:T(1,128)S(1)}, s32[1,256]{1,0:T(1,128)}, u32[]{:S(2)}) copy-start(s32[1,256]{1,0:T(1,128)} %param.13) | copy-start | bytes 3076
  103.9 6.2 %collective-permute-start = (f32[4,128,256]{2,1,0:T(8,128)S(1)}, f32[4,128,256]{2,1,0:T(8,128)S(1)}, u32[]{:S(2)}, u32[]{:S(2)}) collective-permute-start(f32[4,128,256]{2,1,0:T(8,128)S(1)} %get-tuple-element.18), channel_id=1, source_target_pairs={{0,16},{16,0},{32,48},{48,32},{64,80},{80,64},{96,112},{112,96},{1... | collective-permute-start | bytes 1572872 | tf_op jit(solution)/shard_map/ppermute | solution.py:262
  110.3 14.0 %collective-permute-start.3 = (s16[528,256]{1,0:T(8,128)(2,1)S(1)}, s16[528,256]{1,0:T(8,128)(2,1)S(1)}, u32[]{:S(2)}, u32[]{:S(2)}) collective-permute-start(s16[528,256]{1,0:T(8,128)(2,1)S(1)} %chip.1.own), channel_id=1, source_target_pairs={{0,96},{16,112},{32,0},{48,16},{64,32},{80,48},{96,64},{112,80},{1... | collective-permute-start | bytes 811016 | tf_op jit(solution)/shard_map/ppermute | solution.py:282
  113.1 11.1 %collective-permute-start.2 = (s16[528,256]{1,0:T(8,128)(2,1)S(1)}, s16[528,256]{1,0:T(8,128)(2,1)S(1)}, u32[]{:S(2)}, u32[]{:S(2)}) collective-permute-start(s16[528,256]{1,0:T(8,128)(2,1)S(1)} %chip.1.own), channel_id=1, source_target_pairs={{0,64},{16,80},{32,96},{48,112},{64,0},{80,16},{96,32},{112,48},{1... | collective-permute-start | bytes 811016 | tf_op jit(solution)/shard_map/ppermute | solution.py:282
  113.4 15.4 %collective-permute-start.1 = (s16[528,256]{1,0:T(8,128)(2,1)S(1)}, s16[528,256]{1,0:T(8,128)(2,1)S(1)}, u32[]{:S(2)}, u32[]{:S(2)}) collective-permute-start(s16[528,256]{1,0:T(8,128)(2,1)S(1)} %chip.1.own), channel_id=1, source_target_pairs={{0,32},{16,48},{32,64},{48,80},{64,96},{80,112},{96,0},{112,16},{1... | collective-permute-start | bytes 811016 | tf_op jit(solution)/shard_map/ppermute | solution.py:282
  114.1 16.2 %all-to-all-start.3 = ((s16[16,80,256]{2,1,0:T(8,128)(2,1)}), s16[16,80,256]{2,1,0:T(8,128)(2,1)S(1)}, u32[]{:S(2)}, u32[]{:S(2)}) async-start(s16[16,80,256]{2,1,0:T(8,128)(2,1)} %users.3), calls=%async_computation.3 | async-start | bytes 1310720 | tf_op jit(solution)/shard_map/all_to_all | solution.py:285
  129.7 2.1 %collective-permute-start.4 = (f32[4,128,256]{2,1,0:T(8,128)S(1)}, f32[4,128,256]{2,1,0:T(8,128)S(1)}, u32[]{:S(2)}, u32[]{:S(2)}) collective-permute-start(f32[4,128,256]{2,1,0:T(8,128)S(1)} %ring.1.mine), channel_id=1, source_target_pairs={{0,16},{16,0},{32,48},{48,32},{64,80},{80,64},{96,112},{112,96},{1... | collective-permute-start | bytes 1572872 | tf_op jit(solution)/shard_map/ppermute | solution.py:295
